TPU v7x, 32 devices: a whole 2x2x4 slice. The times are simulated.
32 devices in a mesh: rep: 8 (over y, x, core), shard: 4 (over z).
Axes of the slice: x: 2, y: 2, z: 4, core: 2. Of those that a mesh axis runs over, the one named last changes fastest.
Arguments:
- tokens: bfloat16 [16384, 1280], P(('rep', 'shard')), may hold values from -6 to 6
- doc_lengths: int32 [8, 8], P('rep'), may hold values from 1 to 1024, 2048 in all within a row
- cotangent: bfloat16 [16384, 1280], P(('rep', 'shard')), may hold values from -6 to 6
- attn_w: float32 [4, 1280, 1280], P(None, 'shard'), may hold values from -0.15625 to 0.15625
- ffn_w: float32 [3, 5120, 1280], P(None, 'shard'), may hold values from -0.15625 to 0.15625
- attn_m: float32 [4, 1280, 1280], P(None, 'shard'), may hold values from -1.75 to 1.75
- attn_v: float32 [4, 1280, 1280], P(None, 'shard'), may hold values from 0.0564 to 0.228
- ffn_m: float32 [3, 5120, 1280], P(None, 'shard'), may hold values from -1.75 to 1.75
- ffn_v: float32 [3, 5120, 1280], P(None, 'shard'), may hold values from 0.0564 to 0.228
- gains_d: float32 [3, 1280], P(None, 'shard'), as said below
- gains_ff: float32 [2, 5120], P(None, 'shard'), may hold values from 0.25 to 1.75
- gd_m: float32 [3, 1280], P(None, 'shard'), may hold values from -6 to 6
- gd_v: float32 [3, 1280], P(None, 'shard'), may hold values from 0.6312 to 2.52
- gf_m: float32 [2, 5120], P(None, 'shard'), may hold values from -6 to 6
- gf_v: float32 [2, 5120], P(None, 'shard'), may hold values from 0.6312 to 2.52
Outputs:
- output: bfloat16 [16384, 1280], P(('rep', 'shard'))
- grad_tokens: float32 [16384, 1280], P(('rep', 'shard'))
- attn_new: float32 [4, 1280, 1280], P(None, 'shard')
- attn_m_new: float32 [4, 1280, 1280], P(None, 'shard')
- attn_v_new: float32 [4, 1280, 1280], P(None, 'shard')
- ffn_new: float32 [3, 5120, 1280], P(None, 'shard')
- ffn_m_new: float32 [3, 5120, 1280], P(None, 'shard')
- ffn_v_new: float32 [3, 5120, 1280], P(None, 'shard')
- gd_new: float32 [3, 1280], P(None, 'shard')
- gd_m_new: float32 [3, 1280], P(None, 'shard')
- gd_v_new: float32 [3, 1280], P(None, 'shard')
- gf_new: float32 [2, 5120], P(None, 'shard')
- gf_m_new: float32 [2, 5120], P(None, 'shard')
- gf_v_new: float32 [2, 5120], P(None, 'shard')
Inputs may be any that keep to these rules, and one draw needn't show every extreme that they name: `doc_lengths`: each row sums to 2048; its longest document has exactly 1024 tokens. `gains_d`: row 0 (s_qk) lies between 1 and 2, rows 1 and 2 (alpha_A, alpha_M) between 0.2 and 0.6.
All inputs are finite; a program needn't handle non-finite values.
Results may differ from a plain program's by a relative error of at most 0.025.
The roundings to bfloat16 on the way count: a program that leaves them out, or rounds other values in their place, can miss the bound.
Values may be sent and summed in bfloat16 or wider, within the bound.
A program may use at most 448 MiB of HBM per device.

v0:
```python
import functools
import math

import jax
import jax.numpy as jnp
from jax import lax
from jax.experimental import pallas as pl
from jax.experimental.pallas import tpu as pltpu
from jax.sharding import PartitionSpec as P

D = 1280
HEADS = 20
HEAD_DIM = 64
WINDOW = 1024
STEP = 10


SMALL = 1e-06
NEGATIVE = -1e30
BETA_ONE = 0.9
BETA_TWO = 0.95
RATE = 0.02
GAIN_RATE = 1.0
DECAY = 0.1
TINY = 1e-08
F32 = jnp.float32
BF16 = jnp.bfloat16


def from_behind(block, axis, distance):
    devices = range(lax.axis_size(axis))
    route = [(i - distance, i) for i in devices if i - distance in devices]
    return lax.ppermute(block, axis, route)


def rownorm(value):
    factor = lax.rsqrt(jnp.sum(value * value, -1, keepdims=True) + SMALL)
    return (value * factor, factor)


def norm_back(normed, factor, grad):
    return factor * (grad - normed * jnp.sum(normed * grad, -1, keepdims=True))


def adam(weight, grad, first, second, rate, decay):
    first = BETA_ONE * first + (1.0 - BETA_ONE) * grad
    second = BETA_TWO * second + (1.0 - BETA_TWO) * grad * grad
    fix_one = 1.0 - BETA_ONE**STEP
    fix_two = 1.0 - BETA_TWO**STEP
    change = first / fix_one / (jnp.sqrt(second / fix_two) + TINY) + decay * weight
    return (weight - rate * change, first, second)


def dot(a, b):
    return jnp.dot(a, b, preferred_element_type=F32)


def dot_nt(a, b):
    return lax.dot_general(a, b, (((1,), (1,)), ((), ())), preferred_element_type=F32)


def dot_tn(a, b):
    return lax.dot_general(a, b, (((0,), (0,)), ((), ())), preferred_element_type=F32)


def gather_rows(shard_rows):
    reps = lax.axis_size("rep")
    piece = shard_rows.shape[0] // reps
    mine = lax.dynamic_slice_in_dim(shard_rows, lax.axis_index("rep") * piece, piece, 0)
    column = lax.all_gather(mine, "shard", axis=0)
    return lax.all_gather(column, "rep", axis=1)


def reduce_rows(grad):
    part = lax.psum_scatter(grad, "rep", scatter_dimension=0)
    part = lax.psum_scatter(part, "shard", scatter_dimension=0)
    return lax.all_gather(part, "rep", axis=0, tiled=True)


MESH = pl.DeviceIdType.MESH
HALF = 80
RING = 8
HALF_RING = 4


def place():
    rep = lax.axis_index("rep")
    core, chip = lax.rem(rep, 2), rep // 2
    beside, above = chip + 1 - 2 * lax.rem(chip, 2), chip + 2 - 4 * (chip // 2)
    return core, chip, beside, above, 3 - chip


def remote(src, dst, send, recv, rep, shard):
    return pltpu.make_async_remote_copy(
        src_ref=src, dst_ref=dst, send_sem=send, recv_sem=recv,
        device_id=(rep, shard), device_id_type=MESH,
    )


def arrived(ref, sem):
    pltpu.make_async_copy(ref, ref, sem).wait()


def greet(shards):
    rep, line = lax.axis_index("rep"), lax.axis_index("shard")
    barrier = pltpu.get_barrier_semaphore()
    for n in range(1, 8):
        pl.semaphore_signal(barrier, inc=1, device_id=(lax.rem(rep + n, 8), line), device_id_type=MESH)
    for n in range(1, shards):
        pl.semaphore_signal(barrier, inc=1, device_id=(rep, lax.rem(line + n, shards)), device_id_type=MESH)
    pl.semaphore_wait(barrier, 6 + shards)


def add_into(target, sources, rows):
    def step(i, _):
        part = pl.ds(pl.multiple_of(i * 16, 16), 16)
        if len(sources) == 1:
            target[part, :] = target[part, :] + sources[0][part, :]
        else:
            value = target[part, :].astype(F32)
            for source in sources:
                value = value + source[part, :].astype(F32)
            target[part, :] = value.astype(BF16)
        return 0

    lax.fori_loop(0, rows // 16, step, 0, unroll=min(5, rows // 16))


def reduction_scratch(count, shards, rows):
    steps = count * shards
    dma = pltpu.SemaphoreType.DMA
    return [
        pltpu.VMEM((RING, 4, rows, D), BF16),
        pltpu.VMEM((2, 4, rows, D), BF16),
        pltpu.VMEM((HALF_RING, rows, D), BF16),
        pltpu.VMEM((HALF_RING, 2, rows, D), BF16),
        pltpu.VMEM((count, shards + 1, rows, D), BF16),
        dma((2,)), dma(()), dma((steps,)), dma((steps,)), dma((steps, 2)),
        dma((steps,)), dma((steps, 2)), dma((steps,)), dma((count, shards + 1)),
        dma((count,)), dma((count, 7)), dma((count,)), dma(()), pltpu.SemaphoreType.REGULAR,
    ]


def reduction(grads, out, scratch):
    (acc, own, half, piece, below, own_sem, pair_send, pair_recv, half_send, half_recv,
     piece_send, piece_recv, line_send, line_recv, out_send, out_recv, out_local, on_send, credit) = scratch
    count = len(grads)
    rows = own.shape[2]
    shards = below.shape[1] - 1
    core, chip, beside, above, across = place()
    line = lax.axis_index("shard")
    steps = count * shards
    mine, sibling = 2 * chip + core, 2 * chip + 1 - core
    one = piece.at[0, 0]

    def owner(step):
        i = lax.rem(step, shards)
        back = lax.select(i < shards - 1 - line, shards - 1 - i, i - (shards - 1 - line))
        ahead = lax.select(i < line, i, shards - 1 - (i - line))
        other = lax.select(2 * line < shards, back, ahead)
        return lax.select(i == shards - 1, line, other)

    def room(step):
        return acc.at[lax.rem(step, RING)]

    def begin(step):
        slot = lax.rem(step, 2)

        @pl.when(step >= RING)
        def _():
            pl.semaphore_wait(credit, 1)

        for n, grad in enumerate(grads):
            @pl.when(step // shards == n)
            def _(grad=grad):
                remote(grad.at[owner(step), :, 1 - core], room(step), pair_send, pair_recv.at[step], sibling, line).start()
                pltpu.make_async_copy(grad.at[owner(step), :, core], own.at[slot], own_sem.at[slot]).start()

    def first(step):
        slot, part = lax.rem(step, 2), lax.rem(step, HALF_RING)
        total = room(step)
        arrived(own.at[slot], own_sem.at[slot])
        arrived(total, pair_recv.at[step])
        for q in range(4):
            add_into(total.at[q], (own.at[slot, q],), rows)
        remote(total.at[across, pl.ds(0, HALF)], half.at[part, pl.ds(0, HALF)],
               half_send.at[step], half_recv.at[step, 0], 2 * beside + core, line).start()
        remote(total.at[across, pl.ds(HALF, rows - HALF)], half.at[part, pl.ds(HALF, rows - HALF)],
               half_send.at[step], half_recv.at[step, 1], 2 * above + core, line).start()

    def second(step):
        part = lax.rem(step, HALF_RING)
        total = room(step)
        low, high = half.at[part, pl.ds(0, HALF)], half.at[part, pl.ds(HALF, rows - HALF)]
        arrived(low, half_recv.at[step, 0])
        arrived(high, half_recv.at[step, 1])
        add_into(total.at[above, pl.ds(0, HALF)], (low,), HALF)
        add_into(total.at[beside, pl.ds(HALF, rows - HALF)], (high,), rows - HALF)
        remote(total.at[beside], piece.at[part, 0], piece_send.at[step], piece_recv.at[step, 0],
               2 * beside + core, line).start()
        remote(total.at[above], piece.at[part, 1], piece_send.at[step], piece_recv.at[step, 1],
               2 * above + core, line).start()

    def pass_on(step):
        m, target = step // shards, owner(step)

        @pl.when(target > line)
        def _():
            remote(room(step).at[chip], below.at[m, target], line_send.at[step], line_recv.at[m, target],
                   mine, line + 1).start()

        @pl.when(target < line)
        def _():
            slot = lax.select(target == line - 1, shards, target)
            remote(room(step).at[chip], below.at[m, slot], line_send.at[step], line_recv.at[m, slot],
                   mine, line - 1).start()

    def outermost(step):
        target = owner(step)
        return ((target > line) & (line == 0)) | ((target < line) & (line == shards - 1))

    def third(step):
        part = lax.rem(step, HALF_RING)
        for n in range(2):
            arrived(piece.at[part, n], piece_recv.at[step, n])
        add_into(room(step).at[chip], (piece.at[part, 0], piece.at[part, 1]), rows)

        @pl.when(outermost(step))
        def _():
            pass_on(step)

    def along(step):
        m, target = step // shards, owner(step)

        def add_line(slot):
            arrived(below.at[m, slot], line_recv.at[m, slot])
            add_into(room(step).at[chip], (below.at[m, slot],), rows)

        @pl.when(((target >= line) & (line > 0)) | ((target < line) & (line < shards - 1)))
        def _():
            add_line(target)

        @pl.when((target == line) & (line < shards - 1))
        def _():
            add_line(shards)

        @pl.when(jnp.logical_not(outermost(step)))
        def _():
            pass_on(step)

        @pl.when(target == line)
        def _():
            total = room(step).at[chip]
            pltpu.make_async_copy(total, out.at[m, mine], out_local.at[m]).start()
            for n, other in enumerate((2 * beside + core, 2 * above + core, 2 * across + core, sibling)):
                remote(total, out.at[m, mine], out_send.at[m], out_recv.at[m, n], other, line).start()

    def fourth(step):
        m = step // shards
        for n, origin in enumerate((2 * beside + core, 2 * above + core, 2 * across + core)):
            arrived(out.at[m, origin], out_recv.at[m, n])
            remote(out.at[m, origin], out.at[m, origin], on_send, out_recv.at[m, 4 + n], sibling, line).start()

    def retire(step):
        m, target = step // shards, owner(step)
        arrived(one, half_send.at[step])
        arrived(piece.at[0], piece_send.at[step])

        @pl.when(target != line)
        def _():
            arrived(one, line_send.at[step])

        @pl.when(target == line)
        def _():
            arrived(acc.at[0], out_send.at[m])
            arrived(one, out_local.at[m])

        @pl.when(step + RING < steps)
        def _():
            pl.semaphore_signal(credit, inc=1, device_id=(sibling, line), device_id_type=MESH)

    def lead(t):
        @pl.when(t >= 5)
        def _():
            retire(t - 5)

        @pl.when(t == 0)
        def _():
            begin(0)

        @pl.when(t + 1 < steps)
        def _():
            begin(t + 1)

        @pl.when(t < steps)
        def _():
            first(t)

    def follow(t):
        @pl.when((t >= 1) & (t < steps + 1))
        def _():
            second(t - 1)

        @pl.when((t >= 2) & (t < steps + 2))
        def _():
            third(t - 2)

        @pl.when((t >= 3) & (t < steps + 3))
        def _():
            along(t - 3)

        @pl.when((t >= 5) & (lax.rem(t - 5, shards) == shards - 1))
        def _():
            fourth(t - 5)

    def finish():
        for m in range(count):
            for n in range(4):
                arrived(out.at[m, 0], out_recv.at[m, 3 + n])
        arrived(out.at[:, pl.ds(0, 3)], on_send)

    return steps + 5, lead, follow, finish, pair_send


UNITS = 256


def feed_kernel(blocks, mid_ref, middle_ref, cot_ref, alpha_ref, up_scale_ref, gate_scale_ref, wu_ref, wg_ref, wd_ref,
                out_ref, grad_mid_ref, grad_ref, down_ref, up_sum_ref, gate_sum_ref, alpha_sum_ref,
                up_buf, gate_buf, hidden_buf, total, back, grad_hidden_buf, grad_u_buf, grad_g_buf):
    turn = pl.program_id(0)
    after = turn - blocks - 2

    def raw(block):
        up_buf[block] = dot_nt(mid_ref[...], wu_ref[...])
        gate_buf[block] = dot_nt(mid_ref[...], wg_ref[...])

    def activate(block):
        gate = gate_buf[block] * (gate_scale_ref[...] * math.sqrt(D))
        hidden = gate * jax.nn.sigmoid(gate) * (up_buf[block] * up_scale_ref[...])
        hidden_buf[block] = hidden.astype(BF16)

    def project(block, first):
        part = dot(hidden_buf[block], wd_ref[...])
        total[...] = part if first else total[...] + part

    def middle_step():
        alpha = alpha_ref[...]
        rows = total.shape[0]

        def step(i, sums):
            part = pl.ds(pl.multiple_of(i * 32, 32), 32)
            branch, factor = rownorm(total[part, :])
            middle = middle_ref[part, :]
            final, final_factor = rownorm(middle + alpha * (branch - middle))
            out_ref[part, :] = final.astype(BF16)
            grad = norm_back(final, final_factor, cot_ref[part, :].astype(F32))
            grad_mid_ref[part, :] = grad * (1.0 - alpha)
            back[part, :] = norm_back(branch, factor, grad * alpha).astype(BF16)
            return sums + jnp.sum(grad * (branch - middle), 0, keepdims=True)

        alpha_sum_ref[...] = lax.fori_loop(0, rows // 32, step, jnp.zeros((1, D), F32))

    def back_raw():
        grad_hidden_buf[...] = dot_nt(back[...], wd_ref[...])

    def back_activate(block):
        up_scale, gate_scale = up_scale_ref[...], gate_scale_ref[...] * math.sqrt(D)
        grad_hidden = grad_hidden_buf[...]
        up_raw, gate_raw = up_buf[block], gate_buf[block]
        gate = gate_raw * gate_scale
        sigma = jax.nn.sigmoid(gate)
        active = gate * sigma
        upward = up_raw * up_scale
        grad_upward = grad_hidden * active
        grad_gate = grad_hidden * upward * (sigma * (1.0 + gate * (1.0 - sigma)))
        up_sum_ref[...] = jnp.sum(grad_upward * up_raw, 0, keepdims=True)
        gate_sum_ref[...] = jnp.sum(grad_gate * gate_raw, 0, keepdims=True) * math.sqrt(D)
        grad_u_buf[...] = (grad_upward * up_scale).astype(BF16)
        grad_g_buf[...] = (grad_gate * gate_scale).astype(BF16)

    def back_project(block):
        grad_u, grad_g = grad_u_buf[...], grad_g_buf[...]
        grad_ref[0] = dot_tn(grad_u, mid_ref[...]).astype(BF16)
        grad_ref[1] = dot_tn(grad_g, mid_ref[...]).astype(BF16)
        down_ref[...] = dot_tn(hidden_buf[block], back[...]).astype(BF16)
        grad_mid_ref[...] += dot(grad_u, wu_ref[...]) + dot(grad_g, wg_ref[...])

    @pl.when(turn == 0)
    def _():
        raw(0)

    @pl.when(turn == 1)
    def _():
        activate(0)
        raw(1)

    @pl.when(turn == 2)
    def _():
        project(0, True)
        activate(1)
        raw(2)

    @pl.when((turn > 2) & (turn < blocks))
    def _():
        project(turn - 2, False)
        activate(turn - 1)
        raw(turn)

    @pl.when(turn == blocks)
    def _():
        project(turn - 2, False)
        activate(turn - 1)

    @pl.when(turn == blocks + 1)
    def _():
        project(turn - 2, False)
        middle_step()

    @pl.when(after == 0)
    def _():
        back_raw()

    @pl.when(after == 1)
    def _():
        back_activate(0)
        back_raw()

    @pl.when((after > 1) & (after < blocks))
    def _():
        back_project(after - 2)
        back_activate(after - 1)
        back_raw()

    @pl.when(after == blocks)
    def _():
        back_project(after - 2)
        back_activate(after - 1)

    @pl.when(after == blocks + 1)
    def _():
        back_project(after - 2)


def feed_forward(mid_low, middle, cotangent, alpha_ffn, scales, weights, firsts):
    rows = mid_low.shape[0]
    blocks = scales.shape[1] // UNITS
    whole = lambda *shape: pl.BlockSpec(shape, lambda t: (0,) * len(shape))
    half = blocks + 2

    def stage(t, early, late):
        return jnp.clip(lax.select(t < half, t - early, t - half - late), 0, blocks - 1)

    weight = lambda m, early, late: pl.BlockSpec((None, UNITS, D), lambda t: (m, stage(t, early, late), 0))
    done = lambda t, lag: jnp.clip(t - half - lag, 0, blocks - 1)
    units = pl.BlockSpec((1, UNITS), lambda t: (0, done(t, 1)))
    scale = pl.BlockSpec((1, UNITS), lambda t: (0, stage(t, 1, 1)))
    return pl.pallas_call(
        functools.partial(feed_kernel, blocks),
        grid=(2 * half,),
        out_shape=(
            jax.ShapeDtypeStruct((rows, D), BF16),
            jax.ShapeDtypeStruct((rows, D), F32),
            jax.ShapeDtypeStruct((2, blocks * UNITS, D), BF16),
            jax.ShapeDtypeStruct((blocks * UNITS, D), BF16),
            jax.ShapeDtypeStruct((1, blocks * UNITS), F32),
            jax.ShapeDtypeStruct((1, blocks * UNITS), F32),
            jax.ShapeDtypeStruct((1, D), F32),
        ),
        in_specs=[whole(rows, D), whole(rows, D), whole(rows, D), whole(1, D), scale, scale]
        + [weight(firsts[0], 0, 2), weight(firsts[1], 0, 2), weight(firsts[2], 2, 0)],
        out_specs=(
            whole(rows, D), whole(rows, D), pl.BlockSpec((2, UNITS, D), lambda t: (0, done(t, 2), 0)),
            pl.BlockSpec((UNITS, D), lambda t: (done(t, 2), 0)),
            units, units, whole(1, D),
        ),
        scratch_shapes=[
            pltpu.VMEM((blocks, rows, UNITS), F32),
            pltpu.VMEM((blocks, rows, UNITS), F32),
            pltpu.VMEM((blocks, rows, UNITS), BF16),
            pltpu.VMEM((rows, D), F32),
            pltpu.VMEM((rows, D), BF16),
            pltpu.VMEM((rows, UNITS), F32),
            pltpu.VMEM((rows, UNITS), BF16),
            pltpu.VMEM((rows, UNITS), BF16),
        ],
        compiler_params=pltpu.CompilerParams(vmem_limit_bytes=62 * 2**20),
        cost_estimate=pl.CostEstimate(flops=60 * 10**9, bytes_accessed=120 * 10**6, transcendentals=5 * 10**6),
    )(mid_low, middle, cotangent, alpha_ffn, scales[:1], scales[1:], *weights)


def adam_kernel(places, per, *refs):
    grads = refs[:places]
    w_ref, m_ref, v_ref, w_out, m_out, v_out = refs[places:]
    group, piece, _ = w_ref.shape

    def update(g_ref):
        for n in range(group):
            def step(i, _, n=n):
                part = (n, pl.ds(pl.multiple_of(i * 16, 16), 16), slice(None))
                new, first, second = adam(
                    w_ref[part], g_ref[part].astype(F32), m_ref[part], v_ref[part], RATE, DECAY
                )
                w_out[part] = rownorm(new)[0]
                m_out[part] = first
                v_out[part] = second
                return 0

            lax.fori_loop(0, piece // 16, step, 0, unroll=5)

    for n in range(places):
        @pl.when(pl.program_id(0) // per == n)
        def _(n=n):
            update(grads[n])


def adam_rows(weight, grads, first, second):
    places = len(grads)
    _, per, piece, _ = grads[0][0].shape
    group = 2 if per % 2 == 0 else 1
    steps = per // group
    spec = pl.BlockSpec((group, piece, D), lambda p: (p, 0, 0))

    def grad_spec(n, index):
        return pl.BlockSpec(
            (None, group, piece, D), lambda p: (index, jnp.clip(p - n * steps, 0, steps - 1), 0, 0)
        )

    shape = jax.ShapeDtypeStruct((places * per, piece, D), F32)
    news = pl.pallas_call(
        functools.partial(adam_kernel, places, steps),
        grid=(places * steps,),
        out_shape=(shape,) * 3,
        in_specs=[grad_spec(n, index) for n, (_, index) in enumerate(grads)] + [spec] * 3,
        out_specs=(spec,) * 3,
        compiler_params=pltpu.CompilerParams(vmem_limit_bytes=60 * 2**20),
        cost_estimate=pl.CostEstimate(flops=20 * weight.size, bytes_accessed=26 * weight.size, transcendentals=0),
    )(*(array for array, _ in grads), *(old.reshape(shape.shape) for old in (weight, first, second)))
    return tuple(new.reshape(weight.shape) for new in news)


QUERY_BLOCK = 256
PAIR = 2 * HEAD_DIM
PAIRS = HEADS // 2


def head_ones():
    row = lax.broadcasted_iota(jnp.int32, (PAIR, PAIR), 0) // HEAD_DIM
    col = lax.broadcasted_iota(jnp.int32, (PAIR, PAIR), 1) // HEAD_DIM
    return (row == col).astype(F32).astype(BF16)


def head_sum(value, ones):
    high = value.astype(BF16)
    rest = (value - high.astype(F32)).astype(BF16)
    return dot(high, ones) + dot(rest, ones)


def of_head(value, head):
    lane = lax.broadcasted_iota(jnp.int32, value.shape, 1) // HEAD_DIM
    return jnp.where(lane == head, value, jnp.zeros_like(value))


def attend_pair(h_ref, wq_ref, wq2_ref, wk_ref, wk2_ref, wv_ref, wv2_ref, gain_ref, bias_ref, qp_ref, kp_ref, v_ref, o_ref, lse_ref,
                key_buf, query_buf, value_buf):
    cols = h_ref.shape[0]
    rows = qp_ref.shape[0]
    span = bias_ref.shape[1]
    ones = head_ones()
    gain = gain_ref[...]
    weights = jnp.concatenate([wk_ref[...], wk2_ref[...], wv_ref[...], wv2_ref[...]], 0)
    query_weights = jnp.concatenate([wq_ref[...], wq2_ref[...]], 0)

    def project(i, _):
        part = pl.ds(pl.multiple_of(i * QUERY_BLOCK, QUERY_BLOCK), QUERY_BLOCK)
        both = dot_nt(h_ref[part, :], weights)
        keys = both[:, :PAIR]
        kp_ref[part, :] = keys
        factor = lax.rsqrt(head_sum(keys * keys, ones) + SMALL)
        key_buf[part, :] = (keys * factor * gain).astype(BF16)
        values = both[:, PAIR:].astype(BF16)
        v_ref[part, :] = values
        value_buf[part, :PAIR] = values
        value_buf[part, PAIR:] = jnp.ones_like(values)
        return 0

    lax.fori_loop(0, cols // QUERY_BLOCK, project, 0)

    def project_queries(i, _):
        part = pl.ds(pl.multiple_of(i * QUERY_BLOCK, QUERY_BLOCK), QUERY_BLOCK)
        own = pl.ds(pl.multiple_of(cols - rows + i * QUERY_BLOCK, QUERY_BLOCK), QUERY_BLOCK)
        queries = dot_nt(h_ref[own, :], query_weights)
        qp_ref[part, :] = queries
        factor = lax.rsqrt(head_sum(queries * queries, ones) + SMALL)
        scaled = (queries * factor * gain).astype(BF16).astype(F32) * math.sqrt(HEAD_DIM)
        query_buf[part, :] = scaled.astype(BF16)
        return 0

    lax.fori_loop(0, rows // QUERY_BLOCK, project_queries, 0)
    for i in range(rows // QUERY_BLOCK):
        part = pl.ds(i * QUERY_BLOCK, QUERY_BLOCK)
        reach = pl.ds(i * QUERY_BLOCK, span)
        sides = []
        for head in range(2):
            scores = dot_nt(of_head(query_buf[part, :], head), key_buf[reach, :])
            probs = jnp.exp(scores + bias_ref[part, :]).astype(BF16)
            both = dot(probs, value_buf[reach, :])
            total = both[:, PAIR:]
            sides.append(both[:, :PAIR] / total)
            lse_ref[head : head + 1, part] = jnp.log(total).T[:1, :]
        lane = lax.broadcasted_iota(jnp.int32, sides[0].shape, 1)
        o_ref[part, :] = jnp.where(lane < HEAD_DIM, sides[0], sides[1]).astype(BF16)


def back_pair(*refs):
    start, block, finish = back_parts(*refs)
    start()
    for i in range(refs[0].shape[0] // QUERY_BLOCK):
        block(i)
    finish()


def back_parts(qp_ref, kp_ref, v_ref, o_ref, da_ref, wo_ref, wo2_ref, gain_ref, bias_ref, lse_ref,
               dq_ref, dk_ref, dv_ref, sum_ref, key_buf, key_turned, k_total, v_total):
    cols = kp_ref.shape[0]
    rows = qp_ref.shape[0]
    span = bias_ref.shape[1]

    def keys_of(i, _):
        ones, gain = head_ones(), gain_ref[...]
        part = pl.ds(pl.multiple_of(i * QUERY_BLOCK, QUERY_BLOCK), QUERY_BLOCK)
        keys = kp_ref[part, :]
        factor = lax.rsqrt(head_sum(keys * keys, ones) + SMALL)
        low = keys * factor * gain
        key_buf[part, :] = low.astype(BF16)
        key_turned[:, part] = low.T.astype(BF16)
        k_total[part, :] = jnp.zeros_like(keys)
        v_total[part, :] = jnp.zeros_like(keys)
        return 0

    def start():
        lax.fori_loop(0, cols // QUERY_BLOCK, keys_of, 0)

    def block(i):
        ones, gain = head_ones(), gain_ref[...]
        weights = jnp.concatenate([wo_ref[...], wo2_ref[...]], 0)
        part = pl.ds(i * QUERY_BLOCK, QUERY_BLOCK)
        reach = pl.ds(i * QUERY_BLOCK, span)
        queries = qp_ref[part, :]
        factor = lax.rsqrt(head_sum(queries * queries, ones) + SMALL)
        hat = queries * factor
        scaled = ((hat * gain).astype(BF16).astype(F32) * math.sqrt(HEAD_DIM)).astype(BF16)
        back = dot_nt(da_ref[part, :], weights).astype(BF16)
        inner = (back.astype(F32) * o_ref[part, :].astype(F32)).T
        sides = []
        for head in range(2):
            mine = slice(head * HEAD_DIM, (head + 1) * HEAD_DIM)
            query, grad = of_head(scaled, head), of_head(back, head)
            scores = dot_nt(key_buf[reach, :], query)
            probs = jnp.exp(scores + bias_ref[i] - lse_ref[head : head + 1, part])
            v_total[reach, :] += dot(probs.astype(BF16), grad)
            delta = jnp.sum(inner[mine, :], 0, keepdims=True)
            grad_scores = (probs * (dot_nt(v_ref[reach, :], grad) - delta)).astype(BF16)
            k_total[reach, :] += dot(grad_scores, query)
            sides.append(dot(key_turned[mine, reach], grad_scores))
        grad_q = jnp.concatenate(sides, 0).T * math.sqrt(HEAD_DIM)
        sums = jnp.sum(grad_q * hat, 0, keepdims=True)
        if i == 0:
            sum_ref[...] = jnp.broadcast_to(sums, sum_ref.shape)
        else:
            sum_ref[...] += jnp.broadcast_to(sums, sum_ref.shape)
        grad_q = grad_q * gain
        dq_ref[part, :] = (factor * (grad_q - hat * head_sum(hat * grad_q, ones))).astype(BF16)

    def close(i, _):
        ones, gain = head_ones(), gain_ref[...]
        part = pl.ds(pl.multiple_of(i * QUERY_BLOCK, QUERY_BLOCK), QUERY_BLOCK)
        keys = kp_ref[part, :]
        factor = lax.rsqrt(head_sum(keys * keys, ones) + SMALL)
        hat = keys * factor
        grad_k = k_total[part, :]
        sum_ref[...] += jnp.broadcast_to(jnp.sum(grad_k * hat, 0, keepdims=True), sum_ref.shape)
        grad_k = grad_k * gain
        dk_ref[part, :] = (factor * (grad_k - hat * head_sum(hat * grad_k, ones))).astype(BF16)
        dv_ref[part, :] = v_total[part, :].astype(BF16)
        return 0

    def finish():
        lax.fori_loop(0, cols // QUERY_BLOCK, close, 0)

    return start, block, finish


def head_rows(attn_low, matrix, second):
    heads = attn_low.shape[2]

    def index(p):
        head = 2 * p + second
        return (head // heads, matrix, lax.rem(head, heads), 0, 0)

    return pl.BlockSpec((None, None, None, HEAD_DIM, D), index)


def attention_forward(low_all, attn_low, gain_qk, bias, rows):
    cols = low_all.shape[0]
    span = bias.shape[1]
    side = lambda n: pl.BlockSpec((n, PAIR), lambda p: (0, p))
    whole = lambda *shape: pl.BlockSpec(shape, lambda p: (0,) * len(shape))
    return pl.pallas_call(
        attend_pair,
        grid=(PAIRS,),
        out_shape=(
            jax.ShapeDtypeStruct((rows, D), F32),
            jax.ShapeDtypeStruct((cols, D), F32),
            jax.ShapeDtypeStruct((cols, D), BF16),
            jax.ShapeDtypeStruct((rows, D), BF16),
            jax.ShapeDtypeStruct((PAIRS, 8, rows), F32),
        ),
        in_specs=[whole(cols, D)]
        + [head_rows(attn_low, j, second) for j in range(3) for second in range(2)]
        + [side(1), whole(rows, span)],
        out_specs=(side(rows), side(cols), side(cols), side(rows),
                   pl.BlockSpec((None, 8, rows), lambda p: (p, 0, 0))),
        scratch_shapes=[
            pltpu.VMEM((cols, PAIR), BF16),
            pltpu.VMEM((rows, PAIR), BF16),
            pltpu.VMEM((cols, 2 * PAIR), BF16),
        ],
        compiler_params=pltpu.CompilerParams(vmem_limit_bytes=56 * 2**20),
        cost_estimate=pl.CostEstimate(flops=20 * 10**9, bytes_accessed=30 * 10**6, transcendentals=13 * 10**6),
    )(low_all, *[attn_low] * 6, gain_qk, bias)


def attention_backward(q_pre, k_pre, value_all, o_low, grad_spre, attn_low, gain_qk, bias_turned, lse):
    rows, cols = q_pre.shape[0], k_pre.shape[0]
    side = lambda n: pl.BlockSpec((n, PAIR), lambda p: (0, p))
    whole = lambda *shape: pl.BlockSpec(shape, lambda p: (0,) * len(shape))
    stat = pl.BlockSpec((None, 8, rows), lambda p: (p, 0, 0))
    return pl.pallas_call(
        back_pair,
        grid=(PAIRS,),
        out_shape=(
            jax.ShapeDtypeStruct((rows, D), BF16),
            jax.ShapeDtypeStruct((cols, D), BF16),
            jax.ShapeDtypeStruct((cols, D), BF16),
            jax.ShapeDtypeStruct((PAIRS, 8, PAIR), F32),
        ),
        in_specs=[
            side(rows), side(cols), side(cols), side(rows), whole(rows, D),
            head_rows(attn_low, 3, 0), head_rows(attn_low, 3, 1),
            pl.BlockSpec((None, 1, PAIR), lambda p: (p, 0, 0)), whole(*bias_turned.shape), stat,
        ],
        out_specs=(side(rows), side(cols), side(cols), pl.BlockSpec((None, 8, PAIR), lambda p: (p, 0, 0))),
        scratch_shapes=[
            pltpu.VMEM((cols, PAIR), BF16),
            pltpu.VMEM((PAIR, cols), BF16),
            pltpu.VMEM((cols, PAIR), F32),
            pltpu.VMEM((cols, PAIR), F32),
        ],
        compiler_params=pltpu.CompilerParams(vmem_limit_bytes=56 * 2**20),
        cost_estimate=pl.CostEstimate(flops=30 * 10**9, bytes_accessed=40 * 10**6, transcendentals=13 * 10**6),
    )(q_pre, k_pre, value_all, o_low, grad_spre, attn_low, attn_low, gain_qk, bias_turned, lse)


START = 5


def gather_kernel(shards, attn_ref, ffn_ref, gains_ref, tokens_ref, bias_ref,
                  out, gains_out, h_out, qp_out, kp_out, v_out, o_out, lse_ref,
                  wide, low, mine, wide_sem, low_sem, mine_sem, line_send, line_recv, plane_send, beside_recv,
                  above_recv, across_recv, pair_send, pair_recv, gains_send, gains_recv, tokens_send,
                  tokens_recv, local_sem, gains_buf, before, h_buf, load_sem, store_sem,
                  weight_buf, gain_row, qp_buf, kp_buf, v_buf, o_buf, key_buf, query_buf, value_buf):
    core, chip, beside, above, across = place()
    line = lax.axis_index("shard")
    rep = 2 * chip + core
    sibling = 2 * chip + 1 - core
    to_beside, to_above = 2 * beside + core, 2 * above + core
    piece = attn_ref.shape[1]
    rows = tokens_ref.shape[0]
    heads = 2 * piece // HEAD_DIM
    others = shards - 1
    steps = 4 * others
    greet(shards)

    def rows_of(m, shard, rep, start=0, size=None):
        first = pl.multiple_of(rep * piece + start, 16)
        return out.at[m, shard, pl.ds(first, piece if size is None else size)]

    def source(n):
        low_side = 2 * line < shards
        edge = lax.select(low_side, line, shards - 1 - line)
        near = lax.select(lax.rem(n, 2) == 0, edge - 1 - n // 2, edge + 1 + n // 2)
        found = lax.select(n < 2 * edge, near, n + 1)
        return lax.select(low_side, found, shards - 1 - found)

    def own_send(m):
        @pl.when(line < shards - 1)
        def _():
            remote(mine.at[m], rows_of(m, line, rep), line_send, line_recv.at[m, line], rep, line + 1).start()

        @pl.when(line > 0)
        def _():
            remote(mine.at[m], rows_of(m, line, rep), line_send, line_recv.at[m, line], rep, line - 1).start()

    def fetch(index, slot):
        @pl.when(index < 8)
        def _():
            pltpu.make_async_copy(attn_ref.at[lax.rem(index, 8)], wide.at[slot], wide_sem.at[slot]).start()

        @pl.when(index >= 8)
        def _():
            pltpu.make_async_copy(
                ffn_ref.at[jnp.maximum(index // 8 - 1, 0), lax.rem(index, 8)], wide.at[slot], wide_sem.at[slot]
            ).start()

    def store(index, slot):
        return pltpu.make_async_copy(low.at[slot], rows_of(index // 8, line, lax.rem(index, 8)), low_sem.at[slot])

    def lower(src, dst):
        def step(i, _):
            part = pl.ds(pl.multiple_of(i * 32, 32), 32)
            dst[part, :] = src[part, :].astype(BF16)
            return 0

        lax.fori_loop(0, piece // 32, step, 0)

    for n in range(1, shards):
        other = lax.rem(line + n, shards)
        remote(gains_ref, gains_buf.at[line], gains_send, gains_recv.at[line], rep, other).start()
    pltpu.make_async_copy(gains_ref, gains_buf.at[line], local_sem).start()
    own = pl.ds(2 * rows, rows)
    pltpu.make_async_copy(tokens_ref, h_buf.at[own], load_sem.at[0, 0]).start()
    for m in range(4):
        origin = attn_ref.at[rep] if m == 0 else ffn_ref.at[m - 1, rep]
        pltpu.make_async_copy(origin, wide.at[m], mine_sem.at[m]).start()
    for m in range(4):
        arrived(wide.at[m], mine_sem.at[m])
        lower(wide.at[m], mine.at[m])
        if m == 0:
            own_send(0)

            @pl.when(line < shards - 1)
            def _():
                remote(tokens_ref, before.at[1], tokens_send, tokens_recv.at[1], rep, line + 1).start()

    for n in range(2):
        fetch(n, n)

    def norm_rows(source, first):
        def step(i, _):
            at = pl.multiple_of(first + i * 32, 32)
            value = source[pl.ds(pl.multiple_of(i * 32, 32), 32), :].astype(F32)
            h_buf[pl.ds(at, 32), :] = rownorm(value)[0].astype(BF16)
            return 0

        lax.fori_loop(0, rows // 32, step, 0)

    def clear_rows(first):
        h_buf[pl.ds(first, rows), :] = jnp.zeros((rows, D), BF16)

    arrived(h_buf.at[own], load_sem.at[0, 0])
    norm_rows(h_buf.at[own], 2 * rows)

    def loads(p, slot):
        copies = []
        for j in range(3):
            for second in range(2):
                head = 2 * p + second
                first = pl.multiple_of(2 * piece * j + HEAD_DIM * lax.rem(head, heads), HEAD_DIM)
                copies.append(
                    pltpu.make_async_copy(
                        out.at[0, head // heads, pl.ds(first, HEAD_DIM)], weight_buf.at[slot, 2 * j + second],
                        load_sem.at[slot, 2 * j + second],
                    )
                )
        return copies

    def stores(p, slot):
        lanes = pl.ds(pl.multiple_of(p * PAIR, PAIR), PAIR)
        return [
            pltpu.make_async_copy(buf.at[slot], ref.at[:, lanes], store_sem.at[slot, n])
            for n, (ref, buf) in enumerate(((qp_out, qp_buf), (kp_out, kp_buf), (v_out, v_buf), (o_out, o_buf)))
        ]

    def pair(p):
        slot = lax.rem(p, 2)

        @pl.when(p + 1 < PAIRS)
        def _():
            for copy in loads(p + 1, 1 - slot):
                copy.start()

        for copy in loads(p, slot):
            copy.wait()

        @pl.when(p >= 2)
        def _():
            for copy in stores(p - 2, slot):
                copy.wait()

        row = lax.broadcasted_iota(jnp.int32, (8, PAIR), 0)
        left, right = (
            jnp.sum(
                jnp.where(row == lax.rem(2 * p + n, heads), gains_buf[(2 * p + n) // heads, :8, :PAIR], 0.0),
                0, keepdims=True,
            )
            for n in range(2)
        )
        lane = lax.broadcasted_iota(jnp.int32, (1, PAIR), 1)
        gain_row[...] = jnp.where(lane < HEAD_DIM, left, right)
        attend_pair(
            h_buf, *(weight_buf.at[slot, n] for n in range(6)), gain_row, bias_ref, qp_buf.at[slot],
            kp_buf.at[slot], v_buf.at[slot], o_buf.at[slot], lse_ref.at[p], key_buf, query_buf, value_buf,
        )
        for copy in stores(p, slot):
            copy.start()

    def begin(c):
        m, origin = c // others, source(lax.rem(c, others))
        got = rows_of(m, origin, rep)
        arrived(got, line_recv.at[m, origin])

        @pl.when((origin < line) & (line < shards - 1))
        def _():
            remote(got, got, line_send, line_recv.at[m, origin], rep, line + 1).start()

        @pl.when((origin > line) & (line > 0))
        def _():
            remote(got, got, line_send, line_recv.at[m, origin], rep, line - 1).start()

        remote(got, got, plane_send, beside_recv.at[m, origin], to_beside, line).start()
        remote(got, got, plane_send, above_recv.at[m, origin], to_above, line).start()
        remote(got, got, pair_send, pair_recv.at[m], sibling, line).start()

    def middle(c):
        m, origin = c // others, source(lax.rem(c, others))
        got = rows_of(m, origin, to_beside)
        arrived(got, beside_recv.at[m, origin])
        part = rows_of(m, origin, to_beside, 0, HALF)
        remote(part, part, plane_send, across_recv.at[m, origin, 0], to_above, line).start()
        remote(got, got, pair_send, pair_recv.at[m], sibling, line).start()
        got = rows_of(m, origin, to_above)
        arrived(got, above_recv.at[m, origin])
        part = rows_of(m, origin, to_above, HALF, piece - HALF)
        remote(part, part, plane_send, across_recv.at[m, origin, 1], to_beside, line).start()
        remote(got, got, pair_send, pair_recv.at[m], sibling, line).start()

    def last(c):
        m, origin = c // others, source(lax.rem(c, others))
        got = rows_of(m, origin, 2 * across + core)
        arrived(rows_of(m, origin, 2 * across + core, 0, HALF), across_recv.at[m, origin, 0])
        arrived(rows_of(m, origin, 2 * across + core, HALF, piece - HALF), across_recv.at[m, origin, 1])
        remote(got, got, pair_send, pair_recv.at[m], sibling, line).start()

    def local(t):
        for n in range(2):
            index = 2 * t + n
            slot = 2 * lax.rem(t, 2) + n
            arrived(wide.at[slot], wide_sem.at[slot])

            @pl.when(index + 2 < 32)
            def _():
                fetch(index + 2, lax.rem(slot + 2, 4))

            @pl.when(t >= 2)
            def _():
                store(index - 4, slot).wait()

            lower(wide.at[slot], low.at[slot])
            store(index, slot).start()

    def turn(t, _):
        @pl.when((lax.rem(t, others) == 0) & (t // others < 3))
        def _():
            own_send(t // others + 1)

        @pl.when(t < steps)
        def _():
            begin(t)

        @pl.when((t == 1) & (line > 0))
        def _():
            arrived(before.at[1], tokens_recv.at[1])

            @pl.when(line < shards - 1)
            def _():
                remote(before.at[1], before.at[0], tokens_send, tokens_recv.at[0], rep, line + 1).start()

            norm_rows(before.at[1], rows)

        @pl.when((t == 1) & (line == 0))
        def _():
            clear_rows(rows)

        @pl.when((t == 3) & (line > 1))
        def _():
            arrived(before.at[0], tokens_recv.at[0])
            norm_rows(before.at[0], 0)

        @pl.when((t == 3) & (line <= 1))
        def _():
            clear_rows(0)

        @pl.when(t < 2)
        def _():
            local(2 * t)
            local(2 * t + 1)

        @pl.when(t >= 2)
        def _():
            local(t + 2)

        @pl.when(t == START)
        def _():
            pltpu.make_async_copy(gains_ref, gains_buf.at[line], local_sem).wait()
            for n in range(1, shards):
                other = lax.rem(line + n, shards)
                arrived(gains_buf.at[other], gains_recv.at[other])
            arrived(out.at[0, pl.ds(0, others), pl.ds(0, 4 * piece)], pair_recv.at[0])
            for copy in loads(0, 0):
                copy.start()

        early = (t > START + 3).astype(jnp.int32) + (t > START + 6).astype(jnp.int32)
        most = lax.select((t == START + 3) | (t == START + 6), 2, 1)

        def one(n, _):
            pair(t - START + early + n)
            return 0

        lax.fori_loop(0, lax.select((t >= START) & (t < START + PAIRS - 2), most, 0), one, 0)

        @pl.when((t >= 1) & (t < steps + 1))
        def _():
            middle(t - 1)

        @pl.when((t >= 2) & (t < steps + 2))
        def _():
            last(t - 2)

        return 0

    lax.fori_loop(0, 14, turn, 0)
    for n in range(4):
        store(28 + n, n).wait()
    gains_copy = pltpu.make_async_copy(gains_buf, gains_out, local_sem)
    h_copy = pltpu.make_async_copy(h_buf, h_out, load_sem.at[0, 0])
    gains_copy.start()
    h_copy.start()
    for p in (PAIRS - 2, PAIRS - 1):
        for copy in stores(p, p % 2):
            copy.wait()
    for m in range(1, 4):
        arrived(out.at[m, pl.ds(0, others), pl.ds(0, 4 * piece)], pair_recv.at[m])
    gains_copy.wait()
    h_copy.wait()

    @pl.when((line == 1) | (line == shards - 2))
    def _():
        arrived(before, tokens_send)

    @pl.when(line == 0)
    def _():
        arrived(before.at[0], tokens_send)

    @pl.when((line == 0) | (line == shards - 1))
    def _():
        arrived(out.at[:, 0, pl.ds(0, piece)], line_send)

    @pl.when((line > 0) & (line < shards - 1))
    def _():
        arrived(out.at[:, 0, pl.ds(0, 5 * piece)], line_send)

    arrived(out.at[:, pl.ds(0, others), pl.ds(0, 3 * piece)], plane_send)
    arrived(out.at[:, pl.ds(0, others), pl.ds(0, 4 * piece)], pair_send)
    arrived(gains_buf.at[pl.ds(0, others)], gains_send)


def gather_attend(attn_w, ffn_w, gains, tokens, bias, shards):
    piece = attn_w.shape[1]
    rows = tokens.shape[0]
    cols = rows + WINDOW
    any_space = pl.BlockSpec(memory_space=pl.ANY)
    vmem = pl.BlockSpec(memory_space=pltpu.VMEM)
    dma = pltpu.SemaphoreType.DMA
    return pl.pallas_call(
        functools.partial(gather_kernel, shards),
        out_shape=(
            jax.ShapeDtypeStruct((4, shards, 8 * piece, D), BF16),
            jax.ShapeDtypeStruct((shards,) + gains.shape, F32),
            jax.ShapeDtypeStruct((cols, D), BF16),
            jax.ShapeDtypeStruct((rows, D), F32),
            jax.ShapeDtypeStruct((cols, D), F32),
            jax.ShapeDtypeStruct((cols, D), BF16),
            jax.ShapeDtypeStruct((rows, D), BF16),
            jax.ShapeDtypeStruct((PAIRS, 8, rows), F32),
        ),
        in_specs=[any_space] * 4 + [vmem],
        out_specs=(any_space,) * 7 + (vmem,),
        scratch_shapes=[
            pltpu.VMEM((4, piece, D), F32),
            pltpu.VMEM((4, piece, D), BF16),
            pltpu.VMEM((4, piece, D), BF16),
            dma((4,)), dma((4,)), dma((4,)), dma(()), dma((4, shards)), dma(()), dma((4, shards)),
            dma((4, shards)), dma((4, shards, 2)), dma(()), dma((4,)), dma(()), dma((shards,)), dma(()),
            dma((2,)), dma(()),
            pltpu.VMEM((shards,) + gains.shape, F32),
            pltpu.VMEM((2, rows, D), BF16),
            pltpu.VMEM((cols, D), BF16),
            dma((2, 6)), dma((2, 4)),
            pltpu.VMEM((2, 6, HEAD_DIM, D), BF16),
            pltpu.VMEM((1, PAIR), F32),
            pltpu.VMEM((2, rows, PAIR), F32),
            pltpu.VMEM((2, cols, PAIR), F32),
            pltpu.VMEM((2, cols, PAIR), BF16),
            pltpu.VMEM((2, rows, PAIR), BF16),
            pltpu.VMEM((cols, PAIR), BF16),
            pltpu.VMEM((rows, PAIR), BF16),
            pltpu.VMEM((cols, 2 * PAIR), BF16),
        ],
        compiler_params=pltpu.CompilerParams(
            collective_id=3, has_side_effects=True, vmem_limit_bytes=60 * 2**20
        ),
        cost_estimate=pl.CostEstimate(flops=20 * 10**9, bytes_accessed=2 * 10**8, transcendentals=13 * 10**6),
    )(attn_w, ffn_w, gains, tokens, bias)


BACK_BLOCK = 256


def backward_kernel(shards, grads_ref, down_ref, qp_ref, kp_ref, v_ref, o_ref, weight_ref, gains_ref, da_ref, gain_ref,
                    bias_ref, lse_ref, h_ref, out, dq_ref, dk_ref, dv_ref, turned_ref, gains_out, sums_out, back_out,
                    own_out, sums, line_got, plane_got, line_sums, plane_sums, mine_gains, mine_sums, line_send, line_recv, plane_send,
                    plane_recv, back_send, back_recv, *scratch):
    rep, line = lax.axis_index("rep"), lax.axis_index("shard")
    grads = (grads_ref.at[0], grads_ref.at[1], down_ref, turned_ref)
    turns, lead, follow, finish, pair_send = reduction(grads, out, scratch)
    height = weight_ref.shape[2] // 4
    heads = height // HEAD_DIM
    rows, cols = da_ref.shape[0], h_ref.shape[0]
    reach = back_out.shape[0]
    per = rows // BACK_BLOCK
    attended = PAIRS + 1
    dma = pltpu.SemaphoreType.DMA
    greet(shards)

    def attention(qp_buf, kp_buf, v_buf, o_buf, wo_buf, dq_buf, dk_buf, dv_buf, turned_buf, load_sem, store_sem,
                  key_buf, key_turned, k_total, v_total):
        def loads(p, slot):
            lanes = pl.ds(pl.multiple_of(p * PAIR, PAIR), PAIR)
            copies = [
                pltpu.make_async_copy(ref.at[:, lanes], buf.at[slot], load_sem.at[slot, n])
                for n, (ref, buf) in enumerate(((qp_ref, qp_buf), (kp_ref, kp_buf), (v_ref, v_buf), (o_ref, o_buf)))
            ]
            for second in range(2):
                head = 2 * p + second
                first = pl.multiple_of(3 * height + HEAD_DIM * lax.rem(head, heads), HEAD_DIM)
                copies.append(
                    pltpu.make_async_copy(
                        weight_ref.at[0, head // heads, pl.ds(first, HEAD_DIM)], wo_buf.at[slot, second],
                        load_sem.at[slot, 4 + second],
                    )
                )
            return copies

        def lane_stores(p, slot):
            lanes = pl.ds(pl.multiple_of(p * PAIR, PAIR), PAIR)
            return [
                pltpu.make_async_copy(buf.at[slot], ref.at[:, lanes], store_sem.at[slot, n])
                for n, (ref, buf) in enumerate(((dq_ref, dq_buf), (dk_ref, dk_buf), (dv_ref, dv_buf)))
            ]

        def start_stores(p, slot):
            for copy in lane_stores(p, slot):
                copy.start()
            for second in range(2):
                head = 2 * p + second
                for n in range(HEAD_DIM // 32):
                    row = HEAD_DIM * lax.rem(head, heads) + 32 * n
                    place_of = pl.ds(pl.multiple_of(lax.rem(row, height // 2), 32), 32)
                    for j in range(4):
                        pltpu.make_async_copy(
                            turned_buf.at[slot, j, pl.ds(second * HEAD_DIM + 32 * n, 32)],
                            turned_ref.at[head // heads, j, row // (height // 2), place_of], store_sem.at[slot, 3],
                        ).start()

        def wait_stores(p, slot):
            for copy in lane_stores(p, slot):
                copy.wait()
            arrived(turned_buf.at[slot], store_sem.at[slot, 3])

        def pair(p):
            slot = lax.rem(p, 2)

            @pl.when(p + 1 < PAIRS)
            def _():
                for copy in loads(p + 1, 1 - slot):
                    copy.start()

            for copy in loads(p, slot):
                copy.wait()

            @pl.when(p >= 2)
            def _():
                wait_stores(p - 2, slot)

            back_pair(
                qp_buf.at[slot], kp_buf.at[slot], v_buf.at[slot], o_buf.at[slot], da_ref, wo_buf.at[slot, 0],
                wo_buf.at[slot, 1], gain_ref.at[p], bias_ref, lse_ref.at[p], dq_buf.at[slot], dk_buf.at[slot],
                dv_buf.at[slot], sums.at[p], key_buf, key_turned, k_total, v_total,
            )
            turned_buf[slot, 0] = dot_tn(dq_buf[slot], h_ref[pl.ds(cols - rows, rows), :]).astype(BF16)
            turned_buf[slot, 1] = dot_tn(dk_buf[slot], h_ref[...]).astype(BF16)
            turned_buf[slot, 2] = dot_tn(dv_buf[slot], h_ref[...]).astype(BF16)
            turned_buf[slot, 3] = dot_tn(o_buf[slot], da_ref[...]).astype(BF16)
            start_stores(p, slot)

        for copy in loads(0, 0):
            copy.start()

        def step(t, _):
            lead(t)

            @pl.when(t < PAIRS)
            def _():
                pair(t)

            follow(t)
            return 0

        lax.fori_loop(0, attended, step, 0)
        for p in (PAIRS - 2, PAIRS - 1):
            wait_stores(p, p % 2)

    pl.run_scoped(
        attention,
        pltpu.VMEM((2, rows, PAIR), F32),
        pltpu.VMEM((2, cols, PAIR), F32),
        pltpu.VMEM((2, cols, PAIR), BF16),
        pltpu.VMEM((2, rows, PAIR), BF16),
        pltpu.VMEM((2, 2, HEAD_DIM, D), BF16),
        pltpu.VMEM((2, rows, PAIR), BF16),
        pltpu.VMEM((2, cols, PAIR), BF16),
        pltpu.VMEM((2, cols, PAIR), BF16),
        pltpu.VMEM((2, 4, PAIR, D), BF16),
        dma((2, 6)), dma((2, 4)),
        pltpu.VMEM((cols, PAIR), BF16),
        pltpu.VMEM((PAIR, cols), BF16),
        pltpu.VMEM((cols, PAIR), F32),
        pltpu.VMEM((cols, PAIR), F32),
    )

    def inputs(weight_buf, left_buf, parts, weight_sem, left_sem):
        for j in range(3):
            for shard in range(shards):
                pltpu.make_async_copy(
                    weight_ref.at[0, shard, pl.ds(j * height, height)],
                    weight_buf.at[j, pl.ds(shard * height, height)], weight_sem,
                ).start()
        for n in range(1, shards):
            other = lax.rem(line + n, shards)
            remote(gains_ref.at[other], line_got.at[n - 1], line_send.at[0], line_recv.at[0, n - 1], rep, other).start()
            remote(sums, line_sums.at[n - 1], line_send.at[1], line_recv.at[1, n - 1], rep, other).start()

        def lefts(block):
            slot = lax.rem(block, 2)
            part = pl.ds(pl.multiple_of(block * BACK_BLOCK, BACK_BLOCK), BACK_BLOCK)
            return [
                pltpu.make_async_copy(ref.at[part], left_buf.at[slot, n], left_sem.at[slot, n])
                for n, ref in ((1, dk_ref), (2, dv_ref))
            ]

        def own_left(block):
            slot = lax.rem(block, 2)
            part = pl.ds(pl.multiple_of((block - reach * per) * BACK_BLOCK, BACK_BLOCK), BACK_BLOCK)
            return pltpu.make_async_copy(dq_ref.at[part], left_buf.at[slot, 0], left_sem.at[slot, 0])

        def fetch(block):
            for copy in lefts(block):
                copy.start()

            @pl.when(block >= reach * per)
            def _():
                own_left(block).start()

        def product(block):
            slot = lax.rem(block, 2)

            @pl.when(block + 1 < cols // BACK_BLOCK)
            def _():
                fetch(block + 1)

            for copy in lefts(block):
                copy.wait()
            total = dot(left_buf[slot, 1], weight_buf[1]) + dot(left_buf[slot, 2], weight_buf[2])

            @pl.when(block < reach * per)
            def _():
                parts[block] = total.astype(BF16)
                n = block // per
                part = pl.ds(pl.multiple_of(lax.rem(block, per) * BACK_BLOCK, BACK_BLOCK), BACK_BLOCK)

                @pl.when(line >= reach - n)
                def _():
                    remote(parts.at[block], back_out.at[n, part], back_send.at[n], back_recv.at[n], rep,
                           line - (reach - n)).start()

            @pl.when(block >= reach * per)
            def _():
                own_left(block).wait()
                part = pl.ds(pl.multiple_of((block - reach * per) * BACK_BLOCK, BACK_BLOCK), BACK_BLOCK)
                own_out[part, :] = total + dot(left_buf[slot, 0], weight_buf[0])

        fetch(0)

        def step(t, _):
            lead(t)

            @pl.when(t == attended + 1)
            def _():
                arrived(weight_buf, weight_sem)
                for pair_of, (whole, got, got_plane, mine) in enumerate(
                    ((gains_ref.at[line], line_got, plane_got, mine_gains), (sums, line_sums, plane_sums, mine_sums))
                ):
                    total = whole[...]
                    for n in range(shards - 1):
                        arrived(got.at[n], line_recv.at[pair_of, n])
                        total = total + got[n]
                    mine[...] = total
                    for n in range(1, 8):
                        remote(mine, got_plane.at[n - 1], plane_send.at[pair_of], plane_recv.at[pair_of, n - 1],
                               lax.rem(rep + n, 8), line).start()

            @pl.when(t == attended + 3)
            def _():
                for pair_of, (got_plane, mine, result) in enumerate(
                    ((plane_got, mine_gains, gains_out), (plane_sums, mine_sums, sums_out))
                ):
                    total = mine[...]
                    for n in range(7):
                        arrived(got_plane.at[n], plane_recv.at[pair_of, n])
                        total = total + got_plane[n]
                    result[...] = total

            @pl.when((t > attended + 1) & (t < attended + 2 + cols // BACK_BLOCK))
            def _():
                product(t - attended - 2)

            follow(t)
            return 0

        lax.fori_loop(attended, turns, step, 0)
        for n in range(reach):
            @pl.when(line >= reach - n)
            def _(n=n):
                arrived(parts.at[pl.ds(0, per)], back_send.at[n])

            @pl.when(line + reach - n < shards)
            def _(n=n):
                arrived(back_out.at[n], back_recv.at[n])

    pl.run_scoped(
        inputs,
        pltpu.VMEM((3, D, D), BF16),
        pltpu.VMEM((2, 3, BACK_BLOCK, D), BF16),
        pltpu.VMEM((reach * per, BACK_BLOCK, D), BF16),
        dma(()), dma((2, 3)),
    )
    finish()
    arrived(grads_ref, pair_send)
    arrived(line_got, line_send.at[0])
    arrived(line_sums, line_send.at[1])
    arrived(plane_got, plane_send.at[0])
    arrived(plane_sums, plane_send.at[1])


def backward_reduce(grads, down, q_pre, k_pre, value_all, o_low, gathered, gains, grad_spre, gain_qk, bias_turned, lse,
                    low_all):
    _, shards, _, _, rows, _ = grads.shape
    tokens, cols = q_pre.shape[0], k_pre.shape[0]
    reach = (cols - tokens) // tokens
    lines = gains.shape[1:]
    any_space = pl.BlockSpec(memory_space=pl.ANY)
    vmem = pl.BlockSpec(memory_space=pltpu.VMEM)
    dma = pltpu.SemaphoreType.DMA
    return pl.pallas_call(
        functools.partial(backward_kernel, shards),
        out_shape=(
            jax.ShapeDtypeStruct((4, 8, rows, D), BF16),
            jax.ShapeDtypeStruct((tokens, D), BF16),
            jax.ShapeDtypeStruct((cols, D), BF16),
            jax.ShapeDtypeStruct((cols, D), BF16),
            jax.ShapeDtypeStruct(grads.shape[1:], BF16),
            jax.ShapeDtypeStruct(lines, F32),
            jax.ShapeDtypeStruct((PAIRS, 8, PAIR), F32),
            jax.ShapeDtypeStruct((reach, tokens, D), BF16),
            jax.ShapeDtypeStruct((tokens, D), F32),
        ),
        in_specs=[any_space] * 7 + [vmem] * 6,
        out_specs=(any_space,) * 5 + (vmem, vmem, any_space, vmem),
        scratch_shapes=[
            pltpu.VMEM((PAIRS, 8, PAIR), F32),
            pltpu.VMEM((shards - 1,) + lines, F32),
            pltpu.VMEM((7,) + lines, F32),
            pltpu.VMEM((shards - 1, PAIRS, 8, PAIR), F32),
            pltpu.VMEM((7, PAIRS, 8, PAIR), F32),
            pltpu.VMEM(lines, F32),
            pltpu.VMEM((PAIRS, 8, PAIR), F32),
            dma((2,)), dma((2, shards - 1)), dma((2,)), dma((2, 7)), dma((reach,)), dma((reach,)),
        ] + reduction_scratch(4, shards, rows),
        compiler_params=pltpu.CompilerParams(
            collective_id=1, has_side_effects=True, vmem_limit_bytes=63 * 2**20
        ),
        cost_estimate=pl.CostEstimate(flops=55 * 10**9, bytes_accessed=4 * 10**8, transcendentals=13 * 10**6),
    )(grads, down, q_pre, k_pre, value_all, o_low, gathered, gains, grad_spre, gain_qk, bias_turned, lse, low_all)


def body(
    tokens,
    doc_lengths,
    cotangent,
    attn_w,
    ffn_w,
    attn_m,
    attn_v,
    ffn_m,
    ffn_v,
    gains_d,
    gains_ff,
    gd_m,
    gd_v,
    gf_m,
    gf_v,
):
    shards = lax.axis_size("shard")
    reps = lax.axis_size("rep")
    device_index = lax.axis_index("shard")
    rows = tokens.shape[0]
    reach = WINDOW // rows
    cols = (reach + 1) * rows
    attn_rows = attn_w.shape[1]
    ffn_rows = ffn_w.shape[1]
    ffn_all = shards * ffn_rows
    piece = ffn_rows // reps

    lengths_row = doc_lengths[0]
    starts = jnp.cumsum(lengths_row) - lengths_row
    positions = device_index * rows + jnp.arange(rows, dtype=jnp.int32)
    doc_start = jnp.max(
        jnp.where(starts[None, :] <= positions[:, None], starts[None, :], 0), axis=1
    )
    blocks = rows // QUERY_BLOCK
    span = WINDOW + QUERY_BLOCK
    query = jnp.arange(rows, dtype=jnp.int32).reshape(blocks, QUERY_BLOCK)
    lead = query[:, :1] - reach * rows + jnp.arange(span, dtype=jnp.int32)
    ahead = query[:, :, None] - lead[:, None, :]
    floor = (doc_start - device_index * rows).reshape(blocks, QUERY_BLOCK, 1)
    mask = (ahead >= 0) & (ahead < WINDOW) & (lead[:, None, :] >= floor)
    bias = jnp.where(mask, 0.0, NEGATIVE).astype(F32)
    bias_turned = bias.transpose(0, 2, 1)
    bias = bias.reshape(rows, span)
    cut = gains_d.size
    small = jnp.concatenate([gains_d.reshape(-1), gains_ff.reshape(-1)]).astype(BF16)
    normed_in, factor_in = rownorm(tokens.astype(F32))
    fast = reps == 8 and shards == 4 and attn_rows % HEAD_DIM == 0 and reach == 2
    if fast:
        small = small.astype(F32)
        qk_heads = small[:attn_rows].reshape(-1, HEAD_DIM)
        qk_heads = jnp.pad(
            jnp.concatenate([qk_heads, qk_heads], 1), ((0, 8 - qk_heads.shape[0]), (0, D - PAIR))
        )
        small = jnp.pad(small, (0, 8 * D - small.size)).reshape(8, D)
        gathered, small, low_all, q_pre, k_pre, value_all, o_low, lse = gather_attend(
            attn_w.reshape(8, piece, D),
            ffn_w.reshape(3, 8, piece, D),
            jnp.concatenate([qk_heads, small]),
            tokens,
            bias,
            shards,
        )
        small = small[:, 8:].reshape(shards, -1)[:, : cut + gains_ff.size]
        out_low = gathered[0, :, 3 * attn_rows :].reshape(D, D)
        ffn_low = [gathered.reshape(4, ffn_all, D)] * 3
        firsts = (1, 2, 3)
    else:
        attn_low = (
            gather_rows(attn_w.reshape(4 * attn_rows, D).astype(BF16))
            .reshape(shards, 4, attn_rows, D)
            .transpose(1, 0, 2, 3)
            .reshape(1, 4, HEADS, HEAD_DIM, D)
        )
        ffn_low = [gather_rows(ffn_w[m].astype(BF16)).reshape(1, ffn_all, D) for m in range(3)]
        firsts = (0, 0, 0)
        small = lax.all_gather(small, "shard", axis=0).astype(F32)
        query_low, key_low, value_low, out_low = (attn_low[0, j].reshape(D, D) for j in range(4))
    gd_all = small[:, :cut].reshape(shards, 3, -1).transpose(1, 0, 2).reshape(3, D)
    gf_all = small[:, cut:].reshape(shards, 2, ffn_rows).transpose(1, 0, 2).reshape(2, ffn_all)
    gain_qk = gd_all[0]
    alpha_attn = gd_all[1]
    alpha_ffn = gd_all[2]

    if not fast:
        earlier = [from_behind(tokens, "shard", offset) for offset in range(reach, 0, -1)]
        low_all = rownorm(jnp.concatenate(earlier + [tokens], 0).astype(F32))[0].astype(BF16)
        q_pre, k_pre, value_all, o_low, lse = attention_forward(
            low_all, attn_low, gain_qk[None], bias, rows
        )
    in_low = low_all[-rows:]
    side, side_factor = rownorm(dot(o_low, out_low))
    middle, mid_factor = rownorm(normed_in + alpha_attn * (side - normed_in))
    mid_low = middle.astype(BF16)
    output, grad_mid, ffn_grads, down_grads, grad_scale_up, grad_scale_gate, grad_alpha_ffn = feed_forward(
        mid_low, middle, cotangent, alpha_ffn[None], gf_all, ffn_low, firsts
    )
    grad_mixed = norm_back(middle, mid_factor, grad_mid)
    grad_in = grad_mixed * (1.0 - alpha_attn)
    grad_alpha_attn = jnp.sum(grad_mixed * (side - normed_in), 0)
    grad_spre = norm_back(side, side_factor, grad_mixed * alpha_attn).astype(BF16)
    pair_gain = gain_qk.reshape(PAIRS, 1, PAIR)
    grad_gf = jnp.concatenate([grad_scale_up, grad_scale_gate])
    gd_rows = D // shards
    if fast:
        units = (shards, 4, 2, piece, D)
        grad_gd = jnp.stack([grad_alpha_attn, grad_alpha_ffn[0]])
        small = jnp.concatenate(
            [
                grad_gd.reshape(2, shards, gd_rows).transpose(1, 0, 2).reshape(shards, -1),
                grad_gf.reshape(2, shards, ffn_rows).transpose(1, 0, 2).reshape(shards, -1),
            ],
            1,
        )
        small = jnp.pad(small, ((0, 0), (0, 8 * D - small.shape[1]))).reshape(shards, 8, D)
        summed, _, _, _, _, sum_small, sum_qk, back_got, back_own = backward_reduce(
            ffn_grads.reshape((2,) + units), down_grads.reshape(units), q_pre, k_pre, value_all, o_low, gathered,
            small, grad_spre, pair_gain, bias_turned, lse, low_all,
        )
        grad_in = grad_in + back_own
        for n in range(reach):
            sent = device_index + reach - n < shards
            grad_in = grad_in + jnp.where(sent, back_got[n], 0).astype(F32)
        sum_small = sum_small.reshape(-1)
        sum_qk = lax.dynamic_slice_in_dim(sum_qk[:, 0].reshape(D), device_index * gd_rows, gd_rows, 0)
        sum_gd = jnp.concatenate([sum_qk, sum_small[: 2 * gd_rows]]).reshape(3, gd_rows)
        sum_gf = sum_small[2 * gd_rows : 2 * gd_rows + 2 * ffn_rows].reshape(2, ffn_rows)
        attn_sums, ffn_sums = [(summed, 3)], [(summed, 0), (summed, 1), (summed, 2)]
    else:
        grad_qpre, grad_kpre, grad_vpre, gain_sums = attention_backward(
            q_pre, k_pre, value_all, o_low, grad_spre, attn_low, pair_gain, bias_turned, lse
        )
        grad_gain_qk = gain_sums[:, 0].reshape(D)
        back_all = dot(grad_kpre, key_low) + dot(grad_vpre, value_low)
        grad_in = grad_in + dot(grad_qpre, query_low) + back_all[reach * rows :]
        back_parts = back_all[: reach * rows].reshape(reach, rows, D).astype(BF16)
        for n in range(reach):
            grad_in = grad_in + from_behind(back_parts[n], "shard", n - reach).astype(F32)
        attn_grad = jnp.stack(
            [
                dot_tn(grad_qpre, in_low),
                dot_tn(grad_kpre, low_all),
                dot_tn(grad_vpre, low_all),
                dot_tn(o_low, grad_spre),
            ]
        ).astype(BF16)
        attn_grad = attn_grad.reshape(4, shards, attn_rows, D).transpose(1, 0, 2, 3)
        attn_grad = attn_grad.reshape(shards, reps, 4 * attn_rows // reps, D).transpose(1, 0, 2, 3)
        attn_sums = [(reduce_rows(attn_grad).reshape(1, 4, attn_rows, D), 0)]
        ready = (shards, reps, piece, D)
        ffn_sums = [
            (reduce_rows(part.reshape(ready).transpose(1, 0, 2, 3)).reshape(1, 1, ffn_rows, D), 0)
            for part in (ffn_grads[0], ffn_grads[1], down_grads)
        ]
        grad_small = jnp.concatenate(
            [grad_gain_qk, grad_alpha_attn, grad_alpha_ffn[0], grad_gf.reshape(-1)]
        )
        grad_small = lax.psum(grad_small, ("rep", "shard"))
        sum_gd = lax.dynamic_slice_in_dim(
            grad_small[: 3 * D].reshape(3, D), device_index * gd_rows, gd_rows, 1
        )
        sum_gf = lax.dynamic_slice_in_dim(
            grad_small[3 * D :].reshape(2, ffn_all), device_index * ffn_rows, ffn_rows, 1
        )
    grad_tokens = norm_back(normed_in, factor_in, grad_in)

    attn_unit, attn_m_new, attn_v_new = adam_rows(attn_w, attn_sums, attn_m, attn_v)
    ffn_unit, ffn_m_new, ffn_v_new = adam_rows(ffn_w, ffn_sums, ffn_m, ffn_v)
    gd_new, gd_m_new, gd_v_new = adam(gains_d, sum_gd, gd_m, gd_v, GAIN_RATE, 0.0)
    gf_new, gf_m_new, gf_v_new = adam(gains_ff, sum_gf, gf_m, gf_v, GAIN_RATE, 0.0)
    return (
        output,
        grad_tokens,
        attn_unit,
        attn_m_new,
        attn_v_new,
        ffn_unit,
        ffn_m_new,
        ffn_v_new,
        gd_new,
        gd_m_new,
        gd_v_new,
        gf_new,
        gf_m_new,
        gf_v_new,
    )

def solution(mesh):
    return jax.shard_map(
        body,
        mesh=mesh,
        in_specs=(
            P(("rep", "shard"), None),
            P("rep", None),
            P(("rep", "shard"), None),
            P(None, "shard", None),
            P(None, "shard", None),
            P(None, "shard", None),
            P(None, "shard", None),
            P(None, "shard", None),
            P(None, "shard", None),
            P(None, "shard"),
            P(None, "shard"),
            P(None, "shard"),
            P(None, "shard"),
            P(None, "shard"),
            P(None, "shard"),
        ),
        out_specs=(
            P(("rep", "shard"), None),
            P(("rep", "shard"), None),
            P(None, "shard", None),
            P(None, "shard", None),
            P(None, "shard", None),
            P(None, "shard", None),
            P(None, "shard", None),
            P(None, "shard", None),
            P(None, "shard"),
            P(None, "shard"),
            P(None, "shard"),
            P(None, "shard"),
            P(None, "shard"),
            P(None, "shard"),
        ),
        check_vma=False,
    )
```

profile of v0, /device:TPU:17, one launch (start us, length us, event | category | flops | bytes accessed | tf_op | source)
XLA Modules:
  0.0 802.5 jit_solution(2593356059721724349)
XLA Ops:
  0.6 0.7 reshape.236
  1.4 0.8 reshape.235
  3.1 0.8 reduce-window_clone.1
  4.9 2.2 fusion.15.bias_ref
  7.1 216.7 %shard_map.254 = (bf16[4,4,1280,1280]{3,2,1,0:T(8,128)(2,1)}, f32[4,16,1280]{2,1,0:T(8,128)}, bf16[1536,1280]{1,0:T(8,128)(2,1)}, f32[512,1280]{1,0:T(8,128)}, f...) custom-call(f32[8,160,1280]{2,1,0:T(8,128)} %bitcast.76, ...), custom_call_target="tpu_custom_call" | custom-call | flops 20000000000 | bytes 200000000 | tf_op jit(solution)/shard_map/pallas_call | solution.py:1086
  223.9 2.2 slice.79
  226.2 3.4 multiply_reduce_fusion.4
  230.2 2.7 multiply_reduce_fusion.3
  233.0 2.7 fusion.28
  237.7 97.1 %shard_map.255 = (bf16[512,1280]{1,0:T(8,128)(2,1)}, f32[512,1280]{1,0:T(8,128)}, bf16[2,5120,1280]{2,1,0:T(8,128)(2,1)}, bf16[5120,1280]{1,0:T(8,128)(2,1)}, f3...) custom-call(bf16[512,1280]{1,0:T(8,128)(2,1)} %get-tuple-element.80.mid_ref, ...), custom_call_target="tpu_custom_call" | custom-call | flops 60000002048 | bytes 120000000 | tf_op jit(solution)/shard_map/pallas_call | solution.py:458
  334.7 0.8 pad_maximum_fusion
  335.6 0.7 reduce.3
  336.4 3.0 multiply_reduce_fusion.2
  339.7 0.8 copy-done.4
  340.5 4.2 multiply_reduce_fusion
  344.9 0.7 copy.49
  345.6 4.1 multiply_convert_fusion.da_ref
  350.4 1.9 fusion.12.bias_ref
  352.3 374.6 %shard_map.256 = (bf16[4,8,160,1280]{3,2,1,0:T(8,128)(2,1)}, bf16[512,1280]{1,0:T(8,128)(2,1)}, bf16[1536,1280]{1,0:T(8,128)(2,1)}, bf16[1536,1280]{1,0:T(8,128)...) custom-call(bf16[2,4,4,2,160,1280]{5,4,3,2,1,0:T(8,128)(2,1)} %bitca, ...), custom_call_target="tpu_custom_call" | custom-call | flops 54999998464 | bytes 400000000 | tf_op jit(solution)/shard_map/pallas_call | solution.py:1386
  726.9 4.9 fusion.6
  731.8 2.0 fusion.8
  733.8 16.8 %shard_map.257 = (f32[8,160,1280]{2,1,0:T(8,128)}, f32[8,160,1280]{2,1,0:T(8,128)}, f32[8,160,1280]{2,1,0:T(8,128)}) custom-call(bf16[4,8,160,1280]{3,2,1,0:T(8,128)(2,1)} %get-tuple-element.57.refs_0_.refs_1_.refs_2_, f32[8,160,1280]{2,1,0:T(8,128)} %bitcast.77, f32[8,160,1280]{2,1,0:T(8,128)} %bitcast.78, f32[8,160,1280]{2,1,0:T(8,128)} %bitcast.79), custom_call_target="tpu_custom_call" | custom-call | flops 32768000 | bytes 42598400 | tf_op jit(solution)/shard_map/pallas_call | solution.py:530
  750.7 49.0 %shard_map.258 = (f32[24,160,1280]{2,1,0:T(8,128)}, f32[24,160,1280]{2,1,0:T(8,128)}, f32[24,160,1280]{2,1,0:T(8,128)}) custom-call(bf16[4,8,160,1280]{3,2,1,0:T(8,128)(2,1)} %get-tuple-element.57.refs_0_.refs_1_.refs_2_, bf16[4,8,160,1280]{3,2,1,0:T(8,128)(2,1)} %get-tuple-element.57.refs_0_.refs_1_.refs_2_, ...), custom_call_target="tpu_custom_call" | custom-call | flops 98304000 | bytes 127795200 | tf_op jit(solution)/shard_map/pallas_call | solution.py:530
  799.7 0.8 slice_reduce_fusion.3
  (76 shorter events, 7.6 us)
Async XLA Ops:
  223.8 2.3 copy-start.13
  226.1 3.4 copy-start
  226.2 3.7 copy-start.5
  230.2 2.7 copy-start.2
  336.4 3.3 copy-start.3
  336.4 4.1 copy-start.4
  726.9 4.9 copy-start.1
  750.6 49.1 %copy-start.6 = (f32[8,1280]{1,0:T(8,128)S(1)}, f32[8,1280]{1,0:T(8,128)}, u32[]{:S(2)}) copy-start(f32[8,1280]{1,0:T(8,128)} %get-tuple-element.65) | copy-start | bytes 122884
  750.6 50.2 %copy-start.8 = (f32[3,320]{1,0:T(4,128)S(1)}, f32[3,320]{1,0:T(4,128)}, u32[]{:S(2)}) copy-start(f32[3,320]{1,0:T(4,128)} %param.24) | copy-start | bytes 11524
  750.6 50.2 %copy-start.11 = (f32[3,320]{1,0:T(4,128)S(1)}, f32[3,320]{1,0:T(4,128)}, u32[]{:S(2)}) copy-start(f32[3,320]{1,0:T(4,128)} %param.26) | copy-start | bytes 11524
  750.6 50.2 %copy-start.12 = (f32[3,320]{1,0:T(4,128)S(1)}, f32[3,320]{1,0:T(4,128)}, u32[]{:S(2)}) copy-start(f32[3,320]{1,0:T(4,128)} %param.27) | copy-start | bytes 11524
  750.6 50.8 %copy-start.7 = (f32[2,1280]{1,0:T(2,128)S(1)}, f32[2,1280]{1,0:T(2,128)}, u32[]{:S(2)}) copy-start(f32[2,1280]{1,0:T(2,128)} %param.25) | copy-start | bytes 30724
  750.7 50.8 %copy-start.9 = (f32[2,1280]{1,0:T(2,128)S(1)}, f32[2,1280]{1,0:T(2,128)}, u32[]{:S(2)}) copy-start(f32[2,1280]{1,0:T(2,128)} %param.28) | copy-start | bytes 30724
  750.7 50.8 %copy-start.10 = (f32[2,1280]{1,0:T(2,128)S(1)}, f32[2,1280]{1,0:T(2,128)}, u32[]{:S(2)}) copy-start(f32[2,1280]{1,0:T(2,128)} %param.29) | copy-start | bytes 30724
where the time goes:
time: 810 us; the launch traced here: 803 us
  Pallas kernels  754 us (93%)
  other arithmetic  33.5 us (4%)
  local copies, waits for them, and re-layouts  10.1 us (1%)
    pallas_call x1, Pallas kernels, backward_reduce(): pl.pallas_call(functools.partial(backward_kernel, shards), out_shape=(jax...  375 us
    pallas_call x1, Pallas kernels, gather_attend(): pl.pallas_call(functools.partial(gather_kernel, shards), out_shape=(jax.S...  217 us
    pallas_call x1, Pallas kernels, feed_forward(): pl.pallas_call(functools.partial(feed_kernel, blocks), grid=(2 * half,),...  97.1 us
    pallas_call x2, Pallas kernels, adam_rows(): pl.pallas_call(functools.partial(adam_kernel, places, steps), grid=(place...  65.8 us

commit v1 on v0

--- a/solution.py
+++ b/solution.py
@@ -137,7 +137,7 @@
         pltpu.VMEM((count, shards + 1, rows, D), BF16),
         dma((2,)), dma(()), dma((steps,)), dma((steps,)), dma((steps, 2)),
         dma((steps,)), dma((steps, 2)), dma((steps,)), dma((count, shards + 1)),
-        dma((count,)), dma((count, 7)), dma((count,)), dma(()), pltpu.SemaphoreType.REGULAR,
+        dma((count,)), dma((count, 8)), dma((count,)), dma(()), pltpu.SemaphoreType.REGULAR,
     ]
 
 
@@ -252,14 +252,27 @@
         def _():
             total = room(step).at[chip]
             pltpu.make_async_copy(total, out.at[m, mine], out_local.at[m]).start()
-            for n, other in enumerate((2 * beside + core, 2 * above + core, 2 * across + core, sibling)):
+            for n, other in enumerate((2 * beside + core, 2 * above + core, sibling)):
                 remote(total, out.at[m, mine], out_send.at[m], out_recv.at[m, n], other, line).start()
 
     def fourth(step):
         m = step // shards
-        for n, origin in enumerate((2 * beside + core, 2 * above + core, 2 * across + core)):
+        for n, (origin, other, part) in enumerate(
+            (
+                (2 * beside + core, 2 * above + core, pl.ds(0, HALF)),
+                (2 * above + core, 2 * beside + core, pl.ds(HALF, rows - HALF)),
+            )
+        ):
             arrived(out.at[m, origin], out_recv.at[m, n])
-            remote(out.at[m, origin], out.at[m, origin], on_send, out_recv.at[m, 4 + n], sibling, line).start()
+            share = out.at[m, origin, part]
+            remote(share, share, on_send, out_recv.at[m, 3 + n], other, line).start()
+            remote(out.at[m, origin], out.at[m, origin], on_send, out_recv.at[m, 5 + n], sibling, line).start()
+
+    def fifth(step):
+        m, origin = step // shards, 2 * across + core
+        arrived(out.at[m, origin, pl.ds(0, HALF)], out_recv.at[m, 3])
+        arrived(out.at[m, origin, pl.ds(HALF, rows - HALF)], out_recv.at[m, 4])
+        remote(out.at[m, origin], out.at[m, origin], on_send, out_recv.at[m, 7], sibling, line).start()
 
     def retire(step):
         m, target = step // shards, owner(step)
@@ -272,7 +285,7 @@
 
         @pl.when(target == line)
         def _():
-            arrived(acc.at[0], out_send.at[m])
+            arrived(acc.at[0, pl.ds(0, 3)], out_send.at[m])
             arrived(one, out_local.at[m])
 
         @pl.when(step + RING < steps)
@@ -280,9 +293,9 @@
             pl.semaphore_signal(credit, inc=1, device_id=(sibling, line), device_id_type=MESH)
 
     def lead(t):
-        @pl.when(t >= 5)
-        def _():
-            retire(t - 5)
+        @pl.when((t >= 6) & (t < steps + 6))
+        def _():
+            retire(t - 6)
 
         @pl.when(t == 0)
         def _():
@@ -301,25 +314,29 @@
         def _():
             second(t - 1)
 
-        @pl.when((t >= 2) & (t < steps + 2))
-        def _():
-            third(t - 2)
-
         @pl.when((t >= 3) & (t < steps + 3))
         def _():
-            along(t - 3)
-
-        @pl.when((t >= 5) & (lax.rem(t - 5, shards) == shards - 1))
+            third(t - 3)
+
+        @pl.when((t >= 4) & (t < steps + 4))
+        def _():
+            along(t - 4)
+
+        @pl.when((t >= 5) & (t < steps + 5) & (lax.rem(t - 5, shards) == shards - 1))
         def _():
             fourth(t - 5)
+
+        @pl.when((t >= 6) & (t < steps + 6) & (lax.rem(t - 6, shards) == shards - 1))
+        def _():
+            fifth(t - 6)
 
     def finish():
         for m in range(count):
-            for n in range(4):
-                arrived(out.at[m, 0], out_recv.at[m, 3 + n])
-        arrived(out.at[:, pl.ds(0, 3)], on_send)
-
-    return steps + 5, lead, follow, finish, pair_send
+            for n in (2, 5, 6, 7):
+                arrived(out.at[m, 0], out_recv.at[m, n])
+        arrived(out.at[:, pl.ds(0, 4)], on_send)
+
+    return steps + 6, lead, follow, finish, pair_send
 
 
 UNITS = 256

time: 810 us -> 796 us (0.983)
  Pallas kernels: 754 us -> 736 us
    pallas_call x1, Pallas kernels: 375 us -> 357 us  [backward_reduce(): pl.pallas_call(functools.partial(backward_kernel, shards), out_shape=(jax...]
where the time goes in v1:
time: 796 us; the launch traced here: 785 us
  Pallas kernels  736 us (92%)
  other arithmetic  33.5 us (4%)
  local copies, waits for them, and re-layouts  10.1 us (1%)
    pallas_call x1, Pallas kernels, backward_reduce(): pl.pallas_call(functools.partial(backward_kernel, shards), out_shape=(jax...  357 us
    pallas_call x1, Pallas kernels, gather_attend(): pl.pallas_call(functools.partial(gather_kernel, shards), out_shape=(jax.S...  217 us
    pallas_call x1, Pallas kernels, feed_forward(): pl.pallas_call(functools.partial(feed_kernel, blocks), grid=(2 * half,),...  97.1 us
    pallas_call x2, Pallas kernels, adam_rows(): pl.pallas_call(functools.partial(adam_kernel, places, steps), grid=(place...  65.8 us

profile of v1, /device:TPU:17, one launch (start us, length us, event | category | flops | bytes accessed | tf_op | source)
XLA Modules:
  0.0 784.8 jit_solution(441227143179320817)
XLA Ops:
  0.6 0.7 reshape.236
  1.4 0.8 reshape.235
  3.1 0.8 reduce-window_clone.1
  4.9 2.2 fusion.15.bias_ref
  7.1 216.7 %shard_map.254 = (bf16[4,4,1280,1280]{3,2,1,0:T(8,128)(2,1)}, f32[4,16,1280]{2,1,0:T(8,128)}, bf16[1536,1280]{1,0:T(8,128)(2,1)}, f32[512,1280]{1,0:T(8,128)}, f...) custom-call(f32[8,160,1280]{2,1,0:T(8,128)} %bitcast.76, ...), custom_call_target="tpu_custom_call" | custom-call | flops 20000000000 | bytes 200000000 | tf_op jit(solution)/shard_map/pallas_call | solution.py:1103
  223.9 2.2 slice.79
  226.2 3.4 multiply_reduce_fusion.4
  230.2 2.7 multiply_reduce_fusion.3
  233.0 2.7 fusion.28
  237.7 97.1 %shard_map.255 = (bf16[512,1280]{1,0:T(8,128)(2,1)}, f32[512,1280]{1,0:T(8,128)}, bf16[2,5120,1280]{2,1,0:T(8,128)(2,1)}, bf16[5120,1280]{1,0:T(8,128)(2,1)}, f3...) custom-call(bf16[512,1280]{1,0:T(8,128)(2,1)} %get-tuple-element.80.mid_ref, ...), custom_call_target="tpu_custom_call" | custom-call | flops 60000002048 | bytes 120000000 | tf_op jit(solution)/shard_map/pallas_call | solution.py:475
  334.7 0.8 pad_maximum_fusion
  335.6 0.7 reduce.3
  336.4 3.0 multiply_reduce_fusion.2
  339.7 0.8 copy-done.4
  340.5 4.2 multiply_reduce_fusion
  344.9 0.7 copy.49
  345.6 4.1 multiply_convert_fusion.da_ref
  350.4 1.9 fusion.12.bias_ref
  352.3 356.8 %shard_map.256 = (bf16[4,8,160,1280]{3,2,1,0:T(8,128)(2,1)}, bf16[512,1280]{1,0:T(8,128)(2,1)}, bf16[1536,1280]{1,0:T(8,128)(2,1)}, bf16[1536,1280]{1,0:T(8,128)...) custom-call(bf16[2,4,4,2,160,1280]{5,4,3,2,1,0:T(8,128)(2,1)} %bitca, ...), custom_call_target="tpu_custom_call" | custom-call | flops 54999998464 | bytes 400000000 | tf_op jit(solution)/shard_map/pallas_call | solution.py:1403
  709.1 4.9 fusion.6
  714.0 2.0 fusion.8
  716.0 16.8 %shard_map.257 = (f32[8,160,1280]{2,1,0:T(8,128)}, f32[8,160,1280]{2,1,0:T(8,128)}, f32[8,160,1280]{2,1,0:T(8,128)}) custom-call(bf16[4,8,160,1280]{3,2,1,0:T(8,128)(2,1)} %get-tuple-element.57.refs_0_.refs_1_.refs_2_, f32[8,160,1280]{2,1,0:T(8,128)} %bitcast.77, f32[8,160,1280]{2,1,0:T(8,128)} %bitcast.78, f32[8,160,1280]{2,1,0:T(8,128)} %bitcast.79), custom_call_target="tpu_custom_call" | custom-call | flops 32768000 | bytes 42598400 | tf_op jit(solution)/shard_map/pallas_call | solution.py:547
  732.9 49.0 %shard_map.258 = (f32[24,160,1280]{2,1,0:T(8,128)}, f32[24,160,1280]{2,1,0:T(8,128)}, f32[24,160,1280]{2,1,0:T(8,128)}) custom-call(bf16[4,8,160,1280]{3,2,1,0:T(8,128)(2,1)} %get-tuple-element.57.refs_0_.refs_1_.refs_2_, bf16[4,8,160,1280]{3,2,1,0:T(8,128)(2,1)} %get-tuple-element.57.refs_0_.refs_1_.refs_2_, ...), custom_call_target="tpu_custom_call" | custom-call | flops 98304000 | bytes 127795200 | tf_op jit(solution)/shard_map/pallas_call | solution.py:547
  782.0 0.8 slice_reduce_fusion.3
  (76 shorter events, 7.6 us)
Async XLA Ops:
  223.8 2.3 copy-start.13
  226.1 3.4 copy-start
  226.2 3.7 copy-start.5
  230.2 2.7 copy-start.2
  336.4 3.3 copy-start.3
  336.4 4.1 copy-start.4
  709.1 4.9 copy-start.1
  732.8 49.1 %copy-start.6 = (f32[8,1280]{1,0:T(8,128)S(1)}, f32[8,1280]{1,0:T(8,128)}, u32[]{:S(2)}) copy-start(f32[8,1280]{1,0:T(8,128)} %get-tuple-element.65) | copy-start | bytes 122884
  732.9 50.2 %copy-start.8 = (f32[3,320]{1,0:T(4,128)S(1)}, f32[3,320]{1,0:T(4,128)}, u32[]{:S(2)}) copy-start(f32[3,320]{1,0:T(4,128)} %param.24) | copy-start | bytes 11524
  732.9 50.2 %copy-start.11 = (f32[3,320]{1,0:T(4,128)S(1)}, f32[3,320]{1,0:T(4,128)}, u32[]{:S(2)}) copy-start(f32[3,320]{1,0:T(4,128)} %param.26) | copy-start | bytes 11524
  732.9 50.2 %copy-start.12 = (f32[3,320]{1,0:T(4,128)S(1)}, f32[3,320]{1,0:T(4,128)}, u32[]{:S(2)}) copy-start(f32[3,320]{1,0:T(4,128)} %param.27) | copy-start | bytes 11524
  732.9 50.8 %copy-start.7 = (f32[2,1280]{1,0:T(2,128)S(1)}, f32[2,1280]{1,0:T(2,128)}, u32[]{:S(2)}) copy-start(f32[2,1280]{1,0:T(2,128)} %param.25) | copy-start | bytes 30724
  732.9 50.8 %copy-start.9 = (f32[2,1280]{1,0:T(2,128)S(1)}, f32[2,1280]{1,0:T(2,128)}, u32[]{:S(2)}) copy-start(f32[2,1280]{1,0:T(2,128)} %param.28) | copy-start | bytes 30724
  732.9 50.8 %copy-start.10 = (f32[2,1280]{1,0:T(2,128)S(1)}, f32[2,1280]{1,0:T(2,128)}, u32[]{:S(2)}) copy-start(f32[2,1280]{1,0:T(2,128)} %param.29) | copy-start | bytes 30724

commit v2 on v1

--- a/solution.py
+++ b/solution.py
@@ -342,19 +342,55 @@
 UNITS = 256
 
 
-def feed_kernel(blocks, mid_ref, middle_ref, cot_ref, alpha_ref, up_scale_ref, gate_scale_ref, wu_ref, wg_ref, wd_ref,
-                out_ref, grad_mid_ref, grad_ref, down_ref, up_sum_ref, gate_sum_ref, alpha_sum_ref,
-                up_buf, gate_buf, hidden_buf, total, back, grad_hidden_buf, grad_u_buf, grad_g_buf):
+def feed_kernel(blocks, tokens_ref, o_ref, wo_ref, cot_ref, alpha_attn_ref, alpha_ref, up_scale_ref, gate_scale_ref,
+                wu_ref, wg_ref, wd_ref, out_ref, grad_side_ref, grad_in_ref, grad_ref, down_ref, up_sum_ref,
+                gate_sum_ref, alpha_sum_ref, alpha_attn_sum_ref, up_buf, gate_buf, hidden_buf, total, back,
+                grad_hidden_buf, grad_u_buf, grad_g_buf, up_now, gate_now, side_pre, middle_ref, mid_ref, grad_mid_ref):
     turn = pl.program_id(0)
     after = turn - blocks - 2
+    rows = tokens_ref.shape[0]
+
+    def inputs(part):
+        normed = rownorm(tokens_ref[part, :].astype(F32))[0]
+        side, side_factor = rownorm(side_pre[part, :])
+        middle, mid_factor = rownorm(normed + alpha_attn_ref[...] * (side - normed))
+        return normed, side, side_factor, middle, mid_factor
+
+    def start_step():
+        side_pre[...] = dot(o_ref[...], wo_ref[...].reshape(D, D))
+
+        def step(i, _):
+            part = pl.ds(pl.multiple_of(i * 32, 32), 32)
+            middle = inputs(part)[3]
+            middle_ref[part, :] = middle
+            mid_ref[part, :] = middle.astype(BF16)
+            return 0
+
+        lax.fori_loop(0, rows // 32, step, 0)
+
+    def end_step():
+        alpha = alpha_attn_ref[...]
+
+        def step(i, sums):
+            part = pl.ds(pl.multiple_of(i * 32, 32), 32)
+            normed, side, side_factor, middle, mid_factor = inputs(part)
+            grad = norm_back(middle, mid_factor, grad_mid_ref[part, :])
+            grad_in_ref[part, :] = grad * (1.0 - alpha)
+            grad_side_ref[part, :] = norm_back(side, side_factor, grad * alpha).astype(BF16)
+            return sums + jnp.sum(grad * (side - normed), 0, keepdims=True)
+
+        alpha_attn_sum_ref[...] = lax.fori_loop(0, rows // 32, step, jnp.zeros((1, D), F32))
 
     def raw(block):
-        up_buf[block] = dot_nt(mid_ref[...], wu_ref[...])
-        gate_buf[block] = dot_nt(mid_ref[...], wg_ref[...])
+        up_raw, gate_raw = dot_nt(mid_ref[...], wu_ref[...]), dot_nt(mid_ref[...], wg_ref[...])
+        up_now[...] = up_raw
+        gate_now[...] = gate_raw
+        up_buf[block] = up_raw.astype(BF16)
+        gate_buf[block] = gate_raw.astype(BF16)
 
     def activate(block):
-        gate = gate_buf[block] * (gate_scale_ref[...] * math.sqrt(D))
-        hidden = gate * jax.nn.sigmoid(gate) * (up_buf[block] * up_scale_ref[...])
+        gate = gate_now[...] * (gate_scale_ref[...] * math.sqrt(D))
+        hidden = gate * jax.nn.sigmoid(gate) * (up_now[...] * up_scale_ref[...])
         hidden_buf[block] = hidden.astype(BF16)
 
     def project(block, first):
@@ -363,7 +399,6 @@
 
     def middle_step():
         alpha = alpha_ref[...]
-        rows = total.shape[0]
 
         def step(i, sums):
             part = pl.ds(pl.multiple_of(i * 32, 32), 32)
@@ -384,7 +419,7 @@
     def back_activate(block):
         up_scale, gate_scale = up_scale_ref[...], gate_scale_ref[...] * math.sqrt(D)
         grad_hidden = grad_hidden_buf[...]
-        up_raw, gate_raw = up_buf[block], gate_buf[block]
+        up_raw, gate_raw = up_buf[block].astype(F32), gate_buf[block].astype(F32)
         gate = gate_raw * gate_scale
         sigma = jax.nn.sigmoid(gate)
         active = gate * sigma
@@ -405,6 +440,7 @@
 
     @pl.when(turn == 0)
     def _():
+        start_step()
         raw(0)
 
     @pl.when(turn == 1)
@@ -457,12 +493,16 @@
     @pl.when(after == blocks + 1)
     def _():
         back_project(after - 2)
-
-
-def feed_forward(mid_low, middle, cotangent, alpha_ffn, scales, weights, firsts):
-    rows = mid_low.shape[0]
+        end_step()
+
+
+def feed_forward(tokens, o_low, projection, cotangent, alphas, scales, weights, firsts):
+    rows = tokens.shape[0]
+    out_low, place_of = projection
+    _, parts, _, _ = out_low.shape
     blocks = scales.shape[1] // UNITS
     whole = lambda *shape: pl.BlockSpec(shape, lambda t: (0,) * len(shape))
+    held = lambda *shape: pl.BlockSpec(shape, lambda t: (0,) * len(shape), pipeline_mode=pl.Buffered(1))
     half = blocks + 2
 
     def stage(t, early, late):
@@ -477,33 +517,48 @@
         grid=(2 * half,),
         out_shape=(
             jax.ShapeDtypeStruct((rows, D), BF16),
+            jax.ShapeDtypeStruct((rows, D), BF16),
             jax.ShapeDtypeStruct((rows, D), F32),
             jax.ShapeDtypeStruct((2, blocks * UNITS, D), BF16),
             jax.ShapeDtypeStruct((blocks * UNITS, D), BF16),
             jax.ShapeDtypeStruct((1, blocks * UNITS), F32),
             jax.ShapeDtypeStruct((1, blocks * UNITS), F32),
             jax.ShapeDtypeStruct((1, D), F32),
+            jax.ShapeDtypeStruct((1, D), F32),
         ),
-        in_specs=[whole(rows, D), whole(rows, D), whole(rows, D), whole(1, D), scale, scale]
+        in_specs=[
+            held(rows, D),
+            held(rows, D),
+            pl.BlockSpec((None, parts, D // parts, D), lambda t: (0, 0, place_of, 0), pipeline_mode=pl.Buffered(1)),
+            held(rows, D),
+            whole(1, D), whole(1, D), scale, scale,
+        ]
         + [weight(firsts[0], 0, 2), weight(firsts[1], 0, 2), weight(firsts[2], 2, 0)],
         out_specs=(
-            whole(rows, D), whole(rows, D), pl.BlockSpec((2, UNITS, D), lambda t: (0, done(t, 2), 0)),
+            whole(rows, D), whole(rows, D), whole(rows, D),
+            pl.BlockSpec((2, UNITS, D), lambda t: (0, done(t, 2), 0)),
             pl.BlockSpec((UNITS, D), lambda t: (done(t, 2), 0)),
-            units, units, whole(1, D),
+            units, units, whole(1, D), whole(1, D),
         ),
         scratch_shapes=[
-            pltpu.VMEM((blocks, rows, UNITS), F32),
-            pltpu.VMEM((blocks, rows, UNITS), F32),
+            pltpu.VMEM((blocks, rows, UNITS), BF16),
+            pltpu.VMEM((blocks, rows, UNITS), BF16),
             pltpu.VMEM((blocks, rows, UNITS), BF16),
             pltpu.VMEM((rows, D), F32),
             pltpu.VMEM((rows, D), BF16),
             pltpu.VMEM((rows, UNITS), F32),
             pltpu.VMEM((rows, UNITS), BF16),
             pltpu.VMEM((rows, UNITS), BF16),
+            pltpu.VMEM((rows, UNITS), F32),
+            pltpu.VMEM((rows, UNITS), F32),
+            pltpu.VMEM((rows, D), F32),
+            pltpu.VMEM((rows, D), F32),
+            pltpu.VMEM((rows, D), BF16),
+            pltpu.VMEM((rows, D), F32),
         ],
         compiler_params=pltpu.CompilerParams(vmem_limit_bytes=62 * 2**20),
         cost_estimate=pl.CostEstimate(flops=60 * 10**9, bytes_accessed=120 * 10**6, transcendentals=5 * 10**6),
-    )(mid_low, middle, cotangent, alpha_ffn, scales[:1], scales[1:], *weights)
+    )(tokens, o_low, out_low, cotangent, alphas[:1], alphas[1:], scales[:1], scales[1:], *weights)
 
 
 def adam_kernel(places, per, *refs):
@@ -1496,7 +1551,7 @@
             shards,
         )
         small = small[:, 8:].reshape(shards, -1)[:, : cut + gains_ff.size]
-        out_low = gathered[0, :, 3 * attn_rows :].reshape(D, D)
+        projection = (gathered, 3)
         ffn_low = [gathered.reshape(4, ffn_all, D)] * 3
         firsts = (1, 2, 3)
     else:
@@ -1510,11 +1565,10 @@
         firsts = (0, 0, 0)
         small = lax.all_gather(small, "shard", axis=0).astype(F32)
         query_low, key_low, value_low, out_low = (attn_low[0, j].reshape(D, D) for j in range(4))
+        projection = (out_low.reshape(1, 1, D, D), 0)
     gd_all = small[:, :cut].reshape(shards, 3, -1).transpose(1, 0, 2).reshape(3, D)
     gf_all = small[:, cut:].reshape(shards, 2, ffn_rows).transpose(1, 0, 2).reshape(2, ffn_all)
     gain_qk = gd_all[0]
-    alpha_attn = gd_all[1]
-    alpha_ffn = gd_all[2]
 
     if not fast:
         earlier = [from_behind(tokens, "shard", offset) for offset in range(reach, 0, -1)]
@@ -1523,22 +1577,15 @@
             low_all, attn_low, gain_qk[None], bias, rows
         )
     in_low = low_all[-rows:]
-    side, side_factor = rownorm(dot(o_low, out_low))
-    middle, mid_factor = rownorm(normed_in + alpha_attn * (side - normed_in))
-    mid_low = middle.astype(BF16)
-    output, grad_mid, ffn_grads, down_grads, grad_scale_up, grad_scale_gate, grad_alpha_ffn = feed_forward(
-        mid_low, middle, cotangent, alpha_ffn[None], gf_all, ffn_low, firsts
+    output, grad_spre, grad_in, ffn_grads, down_grads, grad_scale_up, grad_scale_gate, grad_alpha_ffn, grad_alpha_attn = (
+        feed_forward(tokens, o_low, projection, cotangent, gd_all[1:], gf_all, ffn_low, firsts)
     )
-    grad_mixed = norm_back(middle, mid_factor, grad_mid)
-    grad_in = grad_mixed * (1.0 - alpha_attn)
-    grad_alpha_attn = jnp.sum(grad_mixed * (side - normed_in), 0)
-    grad_spre = norm_back(side, side_factor, grad_mixed * alpha_attn).astype(BF16)
     pair_gain = gain_qk.reshape(PAIRS, 1, PAIR)
     grad_gf = jnp.concatenate([grad_scale_up, grad_scale_gate])
     gd_rows = D // shards
     if fast:
         units = (shards, 4, 2, piece, D)
-        grad_gd = jnp.stack([grad_alpha_attn, grad_alpha_ffn[0]])
+        grad_gd = jnp.concatenate([grad_alpha_attn, grad_alpha_ffn])
         small = jnp.concatenate(
             [
                 grad_gd.reshape(2, shards, gd_rows).transpose(1, 0, 2).reshape(shards, -1),
@@ -1587,7 +1634,7 @@
             for part in (ffn_grads[0], ffn_grads[1], down_grads)
         ]
         grad_small = jnp.concatenate(
-            [grad_gain_qk, grad_alpha_attn, grad_alpha_ffn[0], grad_gf.reshape(-1)]
+            [grad_gain_qk, grad_alpha_attn[0], grad_alpha_ffn[0], grad_gf.reshape(-1)]
         )
         grad_small = lax.psum(grad_small, ("rep", "shard"))
         sum_gd = lax.dynamic_slice_in_dim(

time: 796 us -> 779 us (0.979)
  other arithmetic: 33.5 us -> 16.2 us
  Pallas kernels: 736 us -> 750 us
    pallas_call x1, Pallas kernels: 97.1 us -> 110 us  [feed_forward(): pl.pallas_call(functools.partial(feed_kernel, blocks), grid=(2 * half,),...]
where the time goes in v2:
time: 779 us; the launch traced here: 774 us
  Pallas kernels  750 us (96%)
  other arithmetic  16.2 us (2%)
    pallas_call x1, Pallas kernels, backward_reduce(): pl.pallas_call(functools.partial(backward_kernel, shards), out_shape=(jax...  357 us
    pallas_call x1, Pallas kernels, gather_attend(): pl.pallas_call(functools.partial(gather_kernel, shards), out_shape=(jax.S...  217 us
    pallas_call x1, Pallas kernels, feed_forward(): pl.pallas_call(functools.partial(feed_kernel, blocks), grid=(2 * half,),...  110 us
    pallas_call x2, Pallas kernels, adam_rows(): pl.pallas_call(functools.partial(adam_kernel, places, steps), grid=(place...  66.2 us

profile of v2, /device:TPU:17, one launch (start us, length us, event | category | flops | bytes accessed | tf_op | source)
XLA Modules:
  0.0 774.5 jit_solution(3152131484666032780)
XLA Ops:
  0.7 0.8 reduce-window_clone.1
  1.5 0.7 subtract_bitcast_fusion
  2.5 2.2 fusion.13.bias_ref
  5.1 0.6 maximum_convert_fusion.gains_ref
  5.8 216.7 %shard_map.254 = (bf16[4,4,1280,1280]{3,2,1,0:T(8,128)(2,1)}, f32[4,16,1280]{2,1,0:T(8,128)}, bf16[1536,1280]{1,0:T(8,128)(2,1)}, f32[512,1280]{1,0:T(8,128)}, f...) custom-call(f32[8,160,1280]{2,1,0:T(8,128)} %bitcast.72, ...), custom_call_target="tpu_custom_call" | custom-call | flops 20000000000 | bytes 200000000 | tf_op jit(solution)/shard_map/pallas_call | solution.py:1158
  222.5 0.9 slice_bitcast_fusion
  223.7 0.7 slice.82.alpha_attn_ref
  224.3 0.7 slice.84.alpha_ref
  225.1 0.6 copy.45
  225.8 0.6 copy.46
  226.4 110.2 %shard_map.255 = (bf16[512,1280]{1,0:T(8,128)(2,1)}, bf16[512,1280]{1,0:T(8,128)(2,1)}, f32[512,1280]{1,0:T(8,128)}, bf16[2,5120,1280]{2,1,0:T(8,128)(2,1)}, bf1...) custom-call(bf16[512,1280]{1,0:T(8,128)(2,1)} %tokens_ref.3, ...), custom_call_target="tpu_custom_call" | custom-call | flops 60000002048 | bytes 120000000 | tf_op jit(solution)/shard_map/pallas_call | solution.py:515
  336.6 0.7 pad_maximum_fusion.1
  337.5 0.8 pad_maximum_fusion
  338.4 0.7 copy.49
  339.1 0.7 reshape_squeeze.6.gain_ref
  339.8 1.9 fusion.10.bias_ref
  341.6 356.8 %shard_map.256 = (bf16[4,8,160,1280]{3,2,1,0:T(8,128)(2,1)}, bf16[512,1280]{1,0:T(8,128)(2,1)}, bf16[1536,1280]{1,0:T(8,128)(2,1)}, bf16[1536,1280]{1,0:T(8,128)...) custom-call(bf16[2,4,4,2,160,1280]{5,4,3,2,1,0:T(8,128)(2,1)} %bitca, ...), custom_call_target="tpu_custom_call" | custom-call | flops 54999998464 | bytes 400000000 | tf_op jit(solution)/shard_map/pallas_call | solution.py:1458
  698.4 0.8 reshape.239
  699.2 0.8 slice_reduce_fusion.3
  700.9 49.3 %shard_map.258 = (f32[24,160,1280]{2,1,0:T(8,128)}, f32[24,160,1280]{2,1,0:T(8,128)}, f32[24,160,1280]{2,1,0:T(8,128)}) custom-call(bf16[4,8,160,1280]{3,2,1,0:T(8,128)(2,1)} %get-tuple-element.61.refs_0_.refs_1_.refs_2_, bf16[4,8,160,1280]{3,2,1,0:T(8,128)(2,1)} %get-tuple-element.61.refs_0_.refs_1_.refs_2_, ...), custom_call_target="tpu_custom_call" | custom-call | flops 98304000 | bytes 127795200 | tf_op jit(solution)/shard_map/pallas_call | solution.py:602
  750.2 16.9 %shard_map.257 = (f32[8,160,1280]{2,1,0:T(8,128)}, f32[8,160,1280]{2,1,0:T(8,128)}, f32[8,160,1280]{2,1,0:T(8,128)}) custom-call(bf16[4,8,160,1280]{3,2,1,0:T(8,128)(2,1)} %get-tuple-element.61.refs_0_.refs_1_.refs_2_, f32[8,160,1280]{2,1,0:T(8,128)} %bitcast.73, f32[8,160,1280]{2,1,0:T(8,128)} %bitcast.74, f32[8,160,1280]{2,1,0:T(8,128)} %bitcast.75), custom_call_target="tpu_custom_call" | custom-call | flops 32768000 | bytes 42598400 | tf_op jit(solution)/shard_map/pallas_call | solution.py:602
  767.4 4.3 fusion.4
  771.8 2.0 fusion.6
  773.8 0.6 add_subtract_fusion
  (53 shorter events, 2.5 us)
Async XLA Ops:
  0.6 4.0 copy-start.1
  0.7 4.0 copy-start.3
  341.6 358.7 %copy-start.6 = (f32[3,320]{1,0:T(4,128)S(1)}, f32[3,320]{1,0:T(4,128)}, u32[]{:S(2)}) copy-start(f32[3,320]{1,0:T(4,128)} %param.26) | copy-start | bytes 11524
  341.6 358.7 %copy-start.7 = (f32[3,320]{1,0:T(4,128)S(1)}, f32[3,320]{1,0:T(4,128)}, u32[]{:S(2)}) copy-start(f32[3,320]{1,0:T(4,128)} %param.27) | copy-start | bytes 11524
  750.2 16.9 %copy-start = (bf16[512,1280]{1,0:T(8,128)(2,1)S(1)}, bf16[512,1280]{1,0:T(8,128)(2,1)}, u32[]{:S(2)}) copy-start(bf16[512,1280]{1,0:T(8,128)(2,1)} %tokens_ref.3) | copy-start | bytes 3932164
  771.8 2.1 copy-start.2
  771.8 2.1 copy-start.4
  771.8 2.1 copy-start.5

commit v3 on v2

--- a/solution.py
+++ b/solution.py
@@ -318,6 +318,7 @@
         def _():
             third(t - 3)
 
+    def settle(t):
         @pl.when((t >= 4) & (t < steps + 4))
         def _():
             along(t - 4)
@@ -336,7 +337,7 @@
                 arrived(out.at[m, 0], out_recv.at[m, n])
         arrived(out.at[:, pl.ds(0, 4)], on_send)
 
-    return steps + 6, lead, follow, finish, pair_send
+    return steps + 6, lead, follow, settle, finish, pair_send
 
 
 UNITS = 256
@@ -366,7 +367,7 @@
             mid_ref[part, :] = middle.astype(BF16)
             return 0
 
-        lax.fori_loop(0, rows // 32, step, 0)
+        lax.fori_loop(0, rows // 32, step, 0, unroll=2)
 
     def end_step():
         alpha = alpha_attn_ref[...]
@@ -379,7 +380,7 @@
             grad_side_ref[part, :] = norm_back(side, side_factor, grad * alpha).astype(BF16)
             return sums + jnp.sum(grad * (side - normed), 0, keepdims=True)
 
-        alpha_attn_sum_ref[...] = lax.fori_loop(0, rows // 32, step, jnp.zeros((1, D), F32))
+        alpha_attn_sum_ref[...] = lax.fori_loop(0, rows // 32, step, jnp.zeros((1, D), F32), unroll=2)
 
     def raw(block):
         up_raw, gate_raw = dot_nt(mid_ref[...], wu_ref[...]), dot_nt(mid_ref[...], wg_ref[...])
@@ -411,7 +412,7 @@
             back[part, :] = norm_back(branch, factor, grad * alpha).astype(BF16)
             return sums + jnp.sum(grad * (branch - middle), 0, keepdims=True)
 
-        alpha_sum_ref[...] = lax.fori_loop(0, rows // 32, step, jnp.zeros((1, D), F32))
+        alpha_sum_ref[...] = lax.fori_loop(0, rows // 32, step, jnp.zeros((1, D), F32), unroll=2)
 
     def back_raw():
         grad_hidden_buf[...] = dot_nt(back[...], wd_ref[...])
@@ -1206,7 +1207,7 @@
                     plane_recv, back_send, back_recv, *scratch):
     rep, line = lax.axis_index("rep"), lax.axis_index("shard")
     grads = (grads_ref.at[0], grads_ref.at[1], down_ref, turned_ref)
-    turns, lead, follow, finish, pair_send = reduction(grads, out, scratch)
+    turns, lead, follow, settle, finish, pair_send = reduction(grads, out, scratch)
     height = weight_ref.shape[2] // 4
     heads = height // HEAD_DIM
     rows, cols = da_ref.shape[0], h_ref.shape[0]
@@ -1261,7 +1262,15 @@
                 copy.wait()
             arrived(turned_buf.at[slot], store_sem.at[slot, 3])
 
-        def pair(p):
+        def stages(p):
+            slot = lax.rem(p, 2)
+            return back_parts(
+                qp_buf.at[slot], kp_buf.at[slot], v_buf.at[slot], o_buf.at[slot], da_ref, wo_buf.at[slot, 0],
+                wo_buf.at[slot, 1], gain_ref.at[p], bias_ref, lse_ref.at[p], dq_buf.at[slot], dk_buf.at[slot],
+                dv_buf.at[slot], sums.at[p], key_buf, key_turned, k_total, v_total,
+            )
+
+        def early(p):
             slot = lax.rem(p, 2)
 
             @pl.when(p + 1 < PAIRS)
@@ -1276,11 +1285,16 @@
             def _():
                 wait_stores(p - 2, slot)
 
-            back_pair(
-                qp_buf.at[slot], kp_buf.at[slot], v_buf.at[slot], o_buf.at[slot], da_ref, wo_buf.at[slot, 0],
-                wo_buf.at[slot, 1], gain_ref.at[p], bias_ref, lse_ref.at[p], dq_buf.at[slot], dk_buf.at[slot],
-                dv_buf.at[slot], sums.at[p], key_buf, key_turned, k_total, v_total,
-            )
+            begin, block, _ = stages(p)
+            begin()
+            block(0)
+
+        def late(p):
+            slot = lax.rem(p, 2)
+            _, block, close = stages(p)
+            for i in range(1, rows // QUERY_BLOCK):
+                block(i)
+            close()
             turned_buf[slot, 0] = dot_tn(dq_buf[slot], h_ref[pl.ds(cols - rows, rows), :]).astype(BF16)
             turned_buf[slot, 1] = dot_tn(dk_buf[slot], h_ref[...]).astype(BF16)
             turned_buf[slot, 2] = dot_tn(dv_buf[slot], h_ref[...]).astype(BF16)
@@ -1295,9 +1309,15 @@
 
             @pl.when(t < PAIRS)
             def _():
-                pair(t)
+                early(t)
 
             follow(t)
+
+            @pl.when(t < PAIRS)
+            def _():
+                late(t)
+
+            settle(t)
             return 0
 
         lax.fori_loop(0, attended, step, 0)
@@ -1419,6 +1439,7 @@
                 product(t - attended - 2)
 
             follow(t)
+            settle(t)
             return 0
 
         lax.fori_loop(attended, turns, step, 0)
@@ -1516,7 +1537,8 @@
     piece = ffn_rows // reps
 
     lengths_row = doc_lengths[0]
-    starts = jnp.cumsum(lengths_row) - lengths_row
+    order = jnp.arange(lengths_row.shape[0])
+    starts = jnp.sum(jnp.where(order[None, :] < order[:, None], lengths_row[None, :], 0), 1)
     positions = device_index * rows + jnp.arange(rows, dtype=jnp.int32)
     doc_start = jnp.max(
         jnp.where(starts[None, :] <= positions[:, None], starts[None, :], 0), axis=1

time: 779 us -> 766 us (0.983)
  Pallas kernels: 750 us -> 737 us
where the time goes in v3:
time: 766 us; the launch traced here: 761 us
  Pallas kernels  737 us (96%)
  other arithmetic  15.5 us (2%)
    pallas_call x1, Pallas kernels, backward_reduce(): pl.pallas_call(functools.partial(backward_kernel, shards), out_shape=(jax...  351 us
    pallas_call x1, Pallas kernels, gather_attend(): pl.pallas_call(functools.partial(gather_kernel, shards), out_shape=(jax.S...  217 us
    pallas_call x1, Pallas kernels, feed_forward(): pl.pallas_call(functools.partial(feed_kernel, blocks), grid=(2 * half,),...  103 us
    pallas_call x2, Pallas kernels, adam_rows(): pl.pallas_call(functools.partial(adam_kernel, places, steps), grid=(place...  66.2 us

profile of v3, /device:TPU:17, one launch (start us, length us, event | category | flops | bytes accessed | tf_op | source)
XLA Modules:
  0.0 761.0 jit_solution(13354586364020352223)
XLA Ops:
  0.7 0.8 select_reduce_fusion.1
  1.8 2.2 fusion.13.bias_ref
  4.4 0.6 maximum_convert_fusion.gains_ref
  5.0 216.7 %shard_map.254 = (bf16[4,4,1280,1280]{3,2,1,0:T(8,128)(2,1)}, f32[4,16,1280]{2,1,0:T(8,128)}, bf16[1536,1280]{1,0:T(8,128)(2,1)}, f32[512,1280]{1,0:T(8,128)}, f...) custom-call(f32[8,160,1280]{2,1,0:T(8,128)} %bitcast.71, ...), custom_call_target="tpu_custom_call" | custom-call | flops 20000000000 | bytes 200000000 | tf_op jit(solution)/shard_map/pallas_call | solution.py:1159
  221.8 0.9 slice_bitcast_fusion
  222.9 0.7 slice.82.alpha_attn_ref
  223.6 0.7 slice.84.alpha_ref
  224.4 0.6 copy.45
  225.0 0.6 copy.46
  225.7 103.0 %shard_map.255 = (bf16[512,1280]{1,0:T(8,128)(2,1)}, bf16[512,1280]{1,0:T(8,128)(2,1)}, f32[512,1280]{1,0:T(8,128)}, bf16[2,5120,1280]{2,1,0:T(8,128)(2,1)}, bf1...) custom-call(bf16[512,1280]{1,0:T(8,128)(2,1)} %tokens_ref.3, ...), custom_call_target="tpu_custom_call" | custom-call | flops 60000002048 | bytes 120000000 | tf_op jit(solution)/shard_map/pallas_call | solution.py:516
  328.7 0.7 pad_maximum_fusion.1
  329.6 0.8 pad_maximum_fusion
  330.5 0.7 copy.49
  331.2 0.7 reshape_squeeze.6.gain_ref
  331.8 1.9 fusion.10.bias_ref
  333.7 351.2 %shard_map.256 = (bf16[4,8,160,1280]{3,2,1,0:T(8,128)(2,1)}, bf16[512,1280]{1,0:T(8,128)(2,1)}, bf16[1536,1280]{1,0:T(8,128)(2,1)}, bf16[1536,1280]{1,0:T(8,128)...) custom-call(bf16[2,4,4,2,160,1280]{5,4,3,2,1,0:T(8,128)(2,1)} %bitca, ...), custom_call_target="tpu_custom_call" | custom-call | flops 54999998464 | bytes 400000000 | tf_op jit(solution)/shard_map/pallas_call | solution.py:1479
  684.9 0.8 reshape.234
  685.7 0.8 slice_reduce_fusion.3
  686.8 0.6 add_subtract_fusion.1
  687.4 49.3 %shard_map.258 = (f32[24,160,1280]{2,1,0:T(8,128)}, f32[24,160,1280]{2,1,0:T(8,128)}, f32[24,160,1280]{2,1,0:T(8,128)}) custom-call(bf16[4,8,160,1280]{3,2,1,0:T(8,128)(2,1)} %get-tuple-element.61.refs_0_.refs_1_.refs_2_, bf16[4,8,160,1280]{3,2,1,0:T(8,128)(2,1)} %get-tuple-element.61.refs_0_.refs_1_.refs_2_, ...), custom_call_target="tpu_custom_call" | custom-call | flops 98304000 | bytes 127795200 | tf_op jit(solution)/shard_map/pallas_call | solution.py:603
  736.6 16.9 %shard_map.257 = (f32[8,160,1280]{2,1,0:T(8,128)}, f32[8,160,1280]{2,1,0:T(8,128)}, f32[8,160,1280]{2,1,0:T(8,128)}) custom-call(bf16[4,8,160,1280]{3,2,1,0:T(8,128)(2,1)} %get-tuple-element.61.refs_0_.refs_1_.refs_2_, f32[8,160,1280]{2,1,0:T(8,128)} %bitcast.72, f32[8,160,1280]{2,1,0:T(8,128)} %bitcast.73, f32[8,160,1280]{2,1,0:T(8,128)} %bitcast.74), custom_call_target="tpu_custom_call" | custom-call | flops 32768000 | bytes 42598400 | tf_op jit(solution)/shard_map/pallas_call | solution.py:603
  753.9 4.3 fusion.4
  758.3 2.0 fusion.6
  760.3 0.6 add_subtract_fusion
  (52 shorter events, 1.9 us)
Async XLA Ops:
  0.6 3.3 copy-start.1
  0.7 3.3 copy-start.3
  333.7 353.1 %copy-start.6 = (f32[3,320]{1,0:T(4,128)S(1)}, f32[3,320]{1,0:T(4,128)}, u32[]{:S(2)}) copy-start(f32[3,320]{1,0:T(4,128)} %param.26) | copy-start | bytes 11524
  333.7 353.1 %copy-start.7 = (f32[3,320]{1,0:T(4,128)S(1)}, f32[3,320]{1,0:T(4,128)}, u32[]{:S(2)}) copy-start(f32[3,320]{1,0:T(4,128)} %param.27) | copy-start | bytes 11524
  736.6 16.9 %copy-start = (bf16[512,1280]{1,0:T(8,128)(2,1)S(1)}, bf16[512,1280]{1,0:T(8,128)(2,1)}, u32[]{:S(2)}) copy-start(bf16[512,1280]{1,0:T(8,128)(2,1)} %tokens_ref.3) | copy-start | bytes 3932164
  758.2 2.1 copy-start.2
  758.3 2.1 copy-start.4
  758.3 2.1 copy-start.5
